TPU v7x, 32 devices: a whole 2x2x4 slice. The times are simulated.
32 devices in a mesh: frame: 4 (over y, core), pack: 8 (over z, x).
Axes of the slice: x: 2, y: 2, z: 4, core: 2. Of those that a mesh axis runs over, the one named last changes fastest.
Arguments:
- tokens: bfloat16 [32, 8, 256, 384], P('pack', 'frame'), may hold values from -6 to 6
- condition: bfloat16 [32, 8, 384], P('pack', 'frame'), may hold values from -6 to 6
- clip_lengths: int32 [32, 4], P('pack'), may hold values from 0 to 8, as said below
- ada_weight: bfloat16 [384, 3456], replicated, may hold values from -0.3125 to 0.3125
- spatial_qkv: bfloat16 [384, 1152], replicated, may hold values from -0.3125 to 0.3125
- spatial_out: bfloat16 [384, 384], replicated, may hold values from -1.25 to 1.25
- temporal_qkv: bfloat16 [384, 1152], replicated, may hold values from -0.3125 to 0.3125
- temporal_out: bfloat16 [384, 384], replicated, may hold values from -0.875 to 0.875
- mlp_up: bfloat16 [384, 1536], replicated, may hold values from -0.3125 to 0.3125
- mlp_down: bfloat16 [1536, 384], replicated, may hold values from -0.15625 to 0.15625
- cotangent: bfloat16 [32, 8, 256, 384], P('pack', 'frame'), may hold values from -6 to 6
Outputs:
- output: bfloat16 [32, 8, 256, 384], P('pack', 'frame')
- tokens_grad: float32 [32, 8, 256, 384], P('pack', 'frame')
- condition_grad: float32 [32, 8, 384], P('pack', 'frame')
- ada_grad: float32 [384, 3456], replicated
- spatial_qkv_grad: float32 [384, 1152], replicated
- spatial_out_grad: float32 [384, 384], replicated
- temporal_qkv_grad: float32 [384, 1152], replicated
- temporal_out_grad: float32 [384, 384], replicated
- mlp_up_grad: float32 [384, 1536], replicated
- mlp_down_grad: float32 [1536, 384], replicated
Inputs may be any that keep to these rules, and one draw needn't show every extreme that they name: `clip_lengths`: row b lists the lengths of the clips of pack b in frame order, each 2, 4 or 8, summing to 8, then zeros. Of the 4 consecutive packs that share an index of pack, at least one is a single clip of 8 frames.
All inputs are finite; a program needn't handle non-finite values.
Results may differ from a plain program's by a relative error of at most 0.02.
The roundings to bfloat16 on the way count: a program that leaves them out, or rounds other values in their place, can miss the bound.
Values may be sent and summed in bfloat16 or wider, within the bound.
No kernel may reach another device: no remote copies, remote signals or barrier semaphores. Data moves between devices by JAX's collectives and lax.ppermute only.
A program may use at most 192 MiB of HBM per device.

v0:
```python
import jax
import jax.numpy as jnp
from jax import lax
from jax.sharding import PartitionSpec as P

D = 384
HEADS = 6
HEAD_DIM = 64
FRAME_DEV = 2


def normalize(values, shift, scale):
    average = jnp.mean(values, axis=-1, keepdims=True)
    centered = values - average
    variance = jnp.mean(centered * centered, axis=-1, keepdims=True)
    return centered * lax.rsqrt(variance + 1e-06) * (1.0 + scale) + shift


def gelu_tanh(values):
    inner = 0.7978845608028654 * (values + 0.044715 * values * values * values)
    return 0.5 * values * (1.0 + jnp.tanh(inner))


def matmul(left, right):
    return jnp.einsum("...i,ij->...j", left, right, preferred_element_type=jnp.float32)


def matmul_back(grad, right):
    return jnp.einsum("...j,ij->...i", grad, right, preferred_element_type=jnp.float32)


def weight_grad(left, grad):
    width_in = left.shape[-1]
    width_out = grad.shape[-1]
    return jnp.einsum(
        "ti,tj->ij",
        left.reshape(-1, width_in),
        grad.reshape(-1, width_out),
        preferred_element_type=jnp.float32,
    )


def split_heads(tensor):
    return tensor.reshape(tensor.shape[:-1] + (HEADS, HEAD_DIM))


def join_heads(tensor):
    return tensor.reshape(tensor.shape[:-2] + (D,))


def attention_scores(query, keys, allowed, forms):
    raw = jnp.einsum(
        forms[0], split_heads(query), split_heads(keys), preferred_element_type=jnp.float32
    ) * HEAD_DIM ** (-0.5)
    return jnp.where(allowed, raw, -1e30)


def attention_forward(packed, allowed, forms):
    query, keys, values = (packed[..., :D], packed[..., D : 2 * D], packed[..., 2 * D :])
    scores = attention_scores(query, keys, allowed, forms)
    highest = jnp.max(scores, axis=-1, keepdims=True)
    total = jnp.log(jnp.sum(jnp.exp(scores - highest), axis=-1, keepdims=True)) + highest
    weights = jnp.exp(scores - total).astype(jnp.bfloat16)
    mixed = jnp.einsum(forms[1], weights, split_heads(values), preferred_element_type=jnp.float32)
    return (join_heads(mixed).astype(jnp.bfloat16), total)


def attention_backward(packed, grad_out, total, allowed, forms):
    query, keys, values = (packed[..., :D], packed[..., D : 2 * D], packed[..., 2 * D :])
    scores = attention_scores(query, keys, allowed, forms)
    probs = jnp.exp(scores - total)
    grad_heads = split_heads(grad_out)
    grad_values = jnp.einsum(
        forms[2], probs.astype(jnp.bfloat16), grad_heads, preferred_element_type=jnp.float32
    )
    grad_probs = jnp.einsum(
        forms[0], grad_heads, split_heads(values), preferred_element_type=jnp.float32
    )
    grad_scores = probs * (grad_probs - jnp.sum(probs * grad_probs, axis=-1, keepdims=True))
    grad_scores = grad_scores.astype(jnp.bfloat16)
    grad_query = jnp.einsum(
        forms[1], grad_scores, split_heads(keys), preferred_element_type=jnp.float32
    ) * HEAD_DIM ** (-0.5)
    grad_keys = jnp.einsum(
        forms[2], grad_scores, split_heads(query), preferred_element_type=jnp.float32
    ) * HEAD_DIM ** (-0.5)
    joined = jnp.concatenate(
        [join_heads(grad_query), join_heads(grad_keys), join_heads(grad_values)], axis=-1
    )
    return joined.astype(jnp.bfloat16)


def local(
    tokens,
    condition,
    clip_lengths,
    ada_weight,
    spatial_qkv,
    spatial_out,
    temporal_qkv,
    temporal_out,
    mlp_up,
    mlp_down,
    cotangent,
):
    frames = FRAME_DEV * lax.axis_size("frame")
    spatial_forms = ("bflhe,bfmhe->bfhlm", "bfhlm,bfmhe->bflhe", "bfhlm,bflhe->bfmhe")
    temporal_forms = ("blphe,bmphe->bphlm", "bphlm,bmphe->blphe", "bphlm,blphe->bmphe")
    ends = jnp.cumsum(clip_lengths, axis=1)
    frame_ids = jnp.arange(frames, dtype=jnp.int32)
    segment = jnp.sum((ends[:, None, :] <= frame_ids[None, :, None]).astype(jnp.int32), axis=2)
    same_clip = (segment[:, :, None] == segment[:, None, :])[:, None, None, :, :]
    inputs = tokens.astype(jnp.float32)
    activated, silu_pull = jax.vjp(jax.nn.silu, condition.astype(jnp.float32))
    activated_low = activated.astype(jnp.bfloat16)
    modulation = matmul(activated_low, ada_weight)
    pieces = [modulation[:, :, None, index * D : (index + 1) * D] for index in range(9)]
    first_full, first_pull = jax.vjp(normalize, inputs, pieces[0], pieces[1])
    first = first_full.astype(jnp.bfloat16)
    qkv_first = matmul(first, spatial_qkv).astype(jnp.bfloat16)
    mixed_first, total_first = attention_forward(qkv_first, True, spatial_forms)
    branch_first = matmul(mixed_first, spatial_out)
    after_first = inputs + pieces[2] * branch_first
    second_full, second_pull = jax.vjp(normalize, after_first, pieces[3], pieces[4])
    second = second_full.astype(jnp.bfloat16)
    qkv_second = matmul(second, temporal_qkv).astype(jnp.bfloat16)
    placed = lax.all_to_all(qkv_second, "frame", split_axis=2, concat_axis=1, tiled=True)
    mixed_placed, total_second = attention_forward(placed, same_clip, temporal_forms)
    mixed_second = lax.all_to_all(mixed_placed, "frame", split_axis=1, concat_axis=2, tiled=True)
    branch_second = matmul(mixed_second, temporal_out)
    after_second = after_first + pieces[5] * branch_second
    third_full, third_pull = jax.vjp(normalize, after_second, pieces[6], pieces[7])
    third = third_full.astype(jnp.bfloat16)
    pre_hidden = matmul(third, mlp_up)
    hidden_full, gelu_pull = jax.vjp(gelu_tanh, pre_hidden)
    hidden = hidden_full.astype(jnp.bfloat16)
    branch_third = matmul(hidden, mlp_down)
    output = (after_second + pieces[8] * branch_third).astype(jnp.bfloat16)
    grad_output = cotangent.astype(jnp.float32)
    grad_gate_third = jnp.sum(grad_output * branch_third, axis=2, keepdims=True)
    grad_branch_third = (pieces[8] * grad_output).astype(jnp.bfloat16)
    grad_down = weight_grad(hidden, grad_branch_third)
    grad_hidden = matmul_back(grad_branch_third, mlp_down)
    grad_pre = gelu_pull(grad_hidden)[0].astype(jnp.bfloat16)
    grad_up = weight_grad(third, grad_pre)
    back_third, grad_shift_third, grad_scale_third = third_pull(matmul_back(grad_pre, mlp_up))
    grad_after_second = grad_output + back_third
    grad_gate_second = jnp.sum(grad_after_second * branch_second, axis=2, keepdims=True)
    grad_branch_second = (pieces[5] * grad_after_second).astype(jnp.bfloat16)
    grad_temporal_out = weight_grad(mixed_second, grad_branch_second)
    grad_mixed_second = matmul_back(grad_branch_second, temporal_out).astype(jnp.bfloat16)
    grad_mixed_placed = lax.all_to_all(
        grad_mixed_second, "frame", split_axis=2, concat_axis=1, tiled=True
    )
    grad_placed = attention_backward(
        placed, grad_mixed_placed, total_second, same_clip, temporal_forms
    )
    grad_qkv_second = lax.all_to_all(grad_placed, "frame", split_axis=1, concat_axis=2, tiled=True)
    grad_temporal_qkv = weight_grad(second, grad_qkv_second)
    grad_second = matmul_back(grad_qkv_second, temporal_qkv)
    back_second, grad_shift_second, grad_scale_second = second_pull(grad_second)
    grad_after_first = grad_after_second + back_second
    grad_gate_first = jnp.sum(grad_after_first * branch_first, axis=2, keepdims=True)
    grad_branch_first = (pieces[2] * grad_after_first).astype(jnp.bfloat16)
    grad_spatial_out = weight_grad(mixed_first, grad_branch_first)
    grad_mixed_first = matmul_back(grad_branch_first, spatial_out).astype(jnp.bfloat16)
    grad_qkv_first = attention_backward(
        qkv_first, grad_mixed_first, total_first, True, spatial_forms
    )
    grad_spatial_qkv = weight_grad(first, grad_qkv_first)
    back_first, grad_shift_first, grad_scale_first = first_pull(
        matmul_back(grad_qkv_first, spatial_qkv)
    )
    grad_inputs = grad_after_first + back_first
    members = (
        grad_shift_first,
        grad_scale_first,
        grad_gate_first,
        grad_shift_second,
        grad_scale_second,
        grad_gate_second,
        grad_shift_third,
        grad_scale_third,
        grad_gate_third,
    )
    grad_modulation = jnp.concatenate([member[:, :, 0, :] for member in members], axis=-1).astype(
        jnp.bfloat16
    )
    grad_ada = weight_grad(activated_low, grad_modulation)
    grad_condition = silu_pull(matmul_back(grad_modulation, ada_weight))[0]
    summed = lax.psum(
        (
            grad_ada,
            grad_spatial_qkv,
            grad_spatial_out,
            grad_temporal_qkv,
            grad_temporal_out,
            grad_up,
            grad_down,
        ),
        ("frame", "pack"),
    )
    return (
        output,
        grad_inputs,
        grad_condition,
        summed[0],
        summed[1],
        summed[2],
        summed[3],
        summed[4],
        summed[5],
        summed[6],
    )


def solution(mesh):
    placed = (
        P("pack", "frame", None, None),
        P("pack", "frame", None),
        P("pack", None),
        P(),
        P(),
        P(),
        P(),
        P(),
        P(),
        P(),
        P("pack", "frame", None, None),
    )
    return jax.shard_map(
        local,
        mesh=mesh,
        in_specs=placed,
        out_specs=(
            P("pack", "frame", None, None),
            P("pack", "frame", None, None),
            P("pack", "frame", None),
            P(),
            P(),
            P(),
            P(),
            P(),
            P(),
            P(),
        ),
        check_vma=False,
    )
```

profile of v0, /device:TPU:0, one launch (start us, length us, event | category | flops | bytes accessed | tf_op | source)
XLA Modules:
  0.0 771.7 jit_solution(512115428928263060)
XLA Ops:
  33.9 7.5 convolution_convert_fusion.5
  52.7 9.4 %copy.277 = bf16[4,2,256,1152]{3,1,0,2:T(2,128)(2,1)} copy(bf16[4,2,256,1152]{3,2,1,0:T(8,128)(2,1)} %convolution_convert_fusion) | data formatting | bytes 9437184 | tf_op jit(solution)/shard_map/convert_element_type | solution.py:126
  67.6 54.1 %all-to-all-done = bf16[4,2,256,1152]{3,1,0,2:T(2,128)(2,1)} async-done(((bf16[4,2,256,1152]{3,1,0,2:T(2,128)(2,1)}), bf16[4,2,256,1152]{3,1,0,2:T(2,128)(2,1)}, u32[]{:S(2)}, u32[]{:S(2)}) %all-to-all-start) | async-done | bytes 4718624 | tf_op jit(solution)/shard_map/all_to_all | solution.py:127
  133.6 5.9 reshape.222
  139.6 8.6 %fusion.9 = (f32[4,64,6,8]{3,2,1,0:T(8,128)S(1)}, f32[4,64,6,8,8]{3,4,2,1,0:T(8,128)S(1)}) fusion(pred[4,8,8]{1,2,0:T(8,128)(4,1)S(1)} %broadcast_compare_fusion, bf16[4,8,64,6,64]{4,3,2,1,0:T(8,128)(2,1)} %reshape.222, bf16[4,8,64,6,64]{4,3,2,1,0:T(8,128)(2,1)} %reshape.221), kind=kOutput, calls=%fused_computation.28 | convolution fusion | flops 12865536 | bytes 3588352 | tf_op jit(solution)/shard_map/blphe,bmphe->bphlm/dot_general | solution.py:52
  158.2 6.3 convert_bitcast_fusion.1
  167.5 6.1 reshape.247
  178.3 20.1 %all-to-all-done.1 = bf16[4,8,64,384]{3,2,0,1:T(8,128)(2,1)} async-done(((bf16[4,8,64,384]{3,2,0,1:T(8,128)(2,1)}), bf16[4,8,64,384]{3,2,0,1:T(8,128)(2,1)}, u32[]{:S(2)}, u32[]{:S(2)}) %all-to-all-start.1) | async-done | bytes 1572896 | tf_op jit(solution)/shard_map/all_to_all | solution.py:129
  209.3 12.7 %fusion.4 = bf16[4,2,256,1536]{3,2,1,0:T(8,128)(2,1)S(1)} fusion(f32[4,2,256,1536]{3,2,1,0:T(8,128)S(1)} %fusion.46, bf16[4,2,256,384]{3,2,1,0:T(8,128)(2,1)S(1)} %copy-done.39, f32[4,2,384]{2,1,0:T(2,128)S(1)} %copy.288, bf16[1536,384]{1,0:T(8,128)(2,1)S(1)} %copy-done.68), kind=kOutput, calls=%fused_computation.7 | convolution fusion | flops 2493775872 | bytes 21639168 | tf_op jit(solution)/shard_map/...j,ij->...i/dot_general | solution.py:29
  233.6 22.5 %all_to_all.69 = bf16[4,2,256,384]{3,1,0,2:T(2,128)(2,1)S(1)} all-to-all(bf16[4,2,256,384]{3,1,0,2:T(2,128)(2,1)S(1)} %copy.291), channel_id=1, replica_groups=mesh['frame'=4,'pack'=8] {'frame'}, dimensions={2} | all-to-all | bytes 3145728 | tf_op jit(solution)/shard_map/all_to_all | solution.py:152
  263.4 14.8 %multiply_reduce_fusion.2 = (f32[4,64,6,8]{3,2,1,0:T(8,128)}, f32[4,64,6,8,8]{3,4,2,1,0:T(8,128)}) fusion(f32[4,64,6,8,8]{3,4,2,1,0:T(8,128)} %copy-done.2, f32[4,64,6,8]{3,2,1,0:T(8,128)} %log_add_fusion, pred[4,8,8]{1,2,0:T(8,128)(4,1)S(1)} %broadcast_compare_fusion, bf16[4,8,64,6,64]{4,3,2,1,0:T(8,128)(2,1)} %reshape.220, ...), kind=kOutput, calls=%fused_computation.21 | convolution fusion | flops 13062144 | bytes 4030720 | tf_op jit(solution)/shard_map/blphe,bmphe->bphlm/dot_general | solution.py:76
  278.3 6.2 multiply_convert_fusion.3
  292.9 7.2 convert_bitcast_fusion
  305.2 6.1 reshape.224
  316.3 6.1 reshape.225
  327.4 6.1 reshape.226
  347.8 7.1 convolution_bitcast_fusion.2
  354.9 10.2 %convolution_bitcast_fusion.1 = f32[1536,384]{1,0:T(8,128)} fusion(bf16[4,2,256,384]{3,2,1,0:T(8,128)(2,1)S(1)} %copy-done.40, f32[4,2,384]{2,1,0:T(2,128)S(1)} %copy.288, f32[4,2,256,1536]{3,2,1,0:T(8,128)} %copy-done.26), kind=kOutput, calls=%fused_computation.76 | convolution fusion | flops 2446589952 | bytes 16527360 | tf_op jit(solution)/shard_map/ti,tj->ij/dot_general | solution.py:35
  365.1 32.5 %all-to-all-done.3 = bf16[4,8,64,1152]{3,2,0,1:T(8,128)(2,1)} async-done(((bf16[4,8,64,1152]{3,2,0,1:T(8,128)(2,1)}), bf16[4,8,64,1152]{3,2,0,1:T(8,128)(2,1)}, u32[]{:S(2)}, u32[]{:S(2)}) %all-to-all-start.3) | async-done | bytes 4718624 | tf_op jit(solution)/shard_map/all_to_all | solution.py:158
  408.0 14.5 %fusion.23 = (bf16[4,2,384]{2,1,0:T(2,128)(2,1)S(1)}, bf16[4,2,384]{2,1,0:T(2,128)(2,1)S(1)}, bf16[4,2,384]{2,1,0:T(2,128)(2,1)S(1)}, f32[4,2,256,384]{3,2,1,0:T(8,128)}, bf16[4,2,256,384]{3,2,1,0:T(8,128)(2,1)}) fusion(bf16[4,2,256,384]{3,2,1,0:T(8,128)(2,1)S(1)} %copy-done.41, f32[4,2,256,384]{3,2,1,0:T(8,128)} %get-tuple-element.119, ...), kind=kOutput, calls=%fused_computation.53 | convolution fusion | flops 2459950080 | bytes 39012352 | tf_op jit(solution)/shard_map/...i,ij->...j/dot_general | solution.py:25
  429.6 13.1 %multiply_reduce_fusion = (f32[4,2,6,256]{3,2,1,0:T(8,128)S(1)}, f32[4,2,6,256,256]{3,4,2,1,0:T(8,128)}) fusion(f32[4,2,6,256,256]{3,4,2,1,0:T(8,128)} %copy-done.1, f32[4,2,6,256]{3,2,1,0:T(8,128)S(1)} %copy-done.33, bf16[4,2,256,6,64]{2,4,3,1,0:T(8,128)(2,1)} %bitcast.167, bf16[4,2,256,6,64]{2,4,3,1,0:T(8,128)(2,1)} %bitcast.181), kind=kOutput, calls=%fused_computation.11 | convolution fusion | flops 415223808 | bytes 28409856 | tf_op jit(solution)/shard_map/bflhe,bfmhe->bfhlm/dot_general | solution.py:76
  442.7 7.1 multiply_convert_fusion
  467.0 6.7 convolution_bitcast_fusion.3
  493.8 258.0 %all-reduce.3.cloned.1.call-done = (f32[384,3456]{1,0:T(8,128)}, f32[384,1152]{1,0:T(8,128)}, f32[384,384]{1,0:T(8,128)}, f32[384,1152]{1,0:T(8,128)}, f32[384,3...) async-done(((f32[384,3456]{1,0:T(8,128)}, f32[384,1152]{1,0:T(8,128)}, f32[384,384]{1,0:T(8,128)}, f32[384,1152]{1,0:T(8,128)}, f32[384,384]{1,0:T(8,128)}, ...) | async-done | bytes 14745616 | tf_op jit(solution)/shard_map/psum | solution.py:191
  (270 shorter events, 207.3 us)
Async XLA Ops:
  31.2 10.1 %copy-start.32 = (f32[4,2,6,256]{3,2,1,0:T(8,128)}, f32[4,2,6,256]{3,2,1,0:T(8,128)S(1)}, u32[]{:S(2)}) copy-start(f32[4,2,6,256]{3,2,1,0:T(8,128)S(1)} %log_add_fusion.1) | copy-start | bytes 147460
  33.8 7.5 copy-start.50
  33.9 7.5 copy-start.10
  33.9 7.5 copy-start.45
  62.1 59.6 %all-to-all-start = ((bf16[4,2,256,1152]{3,1,0,2:T(2,128)(2,1)}), bf16[4,2,256,1152]{3,1,0,2:T(2,128)(2,1)}, u32[]{:S(2)}, u32[]{:S(2)}) async-start(bf16[4,2,256,1152]{3,1,0,2:T(2,128)(2,1)} %copy.277), calls=%async_computation | async-start | bytes 9437184 | tf_op jit(solution)/shard_map/all_to_all | solution.py:127
  173.6 26.6 %copy-start.44 = (bf16[384,384]{1,0:T(8,128)(2,1)S(1)}, bf16[384,384]{1,0:T(8,128)(2,1)}, u32[]{:S(2)}) copy-start(bf16[384,384]{1,0:T(8,128)(2,1)} %param.18) | copy-start | bytes 884740
  173.6 24.8 %all-to-all-start.1 = ((bf16[4,8,64,384]{3,2,0,1:T(8,128)(2,1)}), bf16[4,8,64,384]{3,2,0,1:T(8,128)(2,1)}, u32[]{:S(2)}, u32[]{:S(2)}) async-start(bf16[4,8,64,384]{3,2,0,1:T(8,128)(2,1)} %reshape.247), calls=%async_computation.1 | async-start | bytes 3145728 | tf_op jit(solution)/shard_map/all_to_all | solution.py:129
  203.6 22.8 %copy-start.6 = (f32[4,2,256,384]{3,2,1,0:T(8,128)}, f32[4,2,256,384]{3,2,1,0:T(8,128)S(1)}, u32[]{:S(2)}) copy-start(f32[4,2,256,384]{3,2,1,0:T(8,128)S(1)} %get-tuple-element.93) | copy-start | bytes 9437188
  209.3 12.8 %copy-start.26 = (f32[4,2,256,1536]{3,2,1,0:T(8,128)}, f32[4,2,256,1536]{3,2,1,0:T(8,128)S(1)}, u32[]{:S(2)}) copy-start(f32[4,2,256,1536]{3,2,1,0:T(8,128)S(1)} %fusion.46) | copy-start | bytes 37748740
  278.3 14.6 %slice-start.3 = ((s8[6291456]{0:T(1024)(128)(4,1)}), s8[4194304]{0:T(1024)(128)(4,1)S(1)}, s32[]{:S(2)}) async-start(s8[6291456]{0:T(1024)(128)(4,1)} %bitcast.165), calls=%async_computation.8 | async-start | bytes 8388608
  284.7 8.2 %slice-start.4 = ((s8[6291456]{0:T(1024)(128)(4,1)}), s8[2097152]{0:T(1024)(128)(4,1)S(1)}, s32[]{:S(2)}) async-start(s8[6291456]{0:T(1024)(128)(4,1)} %bitcast.165), calls=%async_computation.9 | async-start | bytes 4194304
  338.7 58.9 %all-to-all-start.3 = ((bf16[4,8,64,1152]{3,2,0,1:T(8,128)(2,1)}), bf16[4,8,64,1152]{3,2,0,1:T(8,128)(2,1)}, u32[]{:S(2)}, u32[]{:S(2)}) async-start(bf16[4,8,64,1152]{3,2,0,1:T(8,128)(2,1)} %copy.302), calls=%async_computation.3 | async-start | bytes 9437184 | tf_op jit(solution)/shard_map/all_to_all | solution.py:158
  343.7 408.1 %all-reduce.3.cloned.1.call-start = ((), (), s32[]{:S(2)}) async-start(), calls=%async_computation.4 | async-start | bytes 29491200 | tf_op jit(solution)/shard_map/psum | solution.py:191
  347.8 7.1 copy-start.40
  408.0 14.5 %copy-start.46 = (bf16[384,384]{1,0:T(8,128)(2,1)S(1)}, bf16[384,384]{1,0:T(8,128)(2,1)}, u32[]{:S(2)}) copy-start(bf16[384,384]{1,0:T(8,128)(2,1)} %param.16) | copy-start | bytes 884740
  408.0 14.5 %copy-start.51 = (f32[4,2,384]{2,1,0:T(2,128)S(1)}, f32[4,2,384]{2,1,0:T(2,128)}, u32[]{:S(2)}) copy-start(f32[4,2,384]{2,1,0:T(2,128)} %copy-done.50) | copy-start | bytes 36868
  422.5 7.0 copy-start.33
  429.5 13.2 %slice-start = ((s8[12582912]{0:T(1024)(128)(4,1)}), s8[4194304]{0:T(1024)(128)(4,1)S(1)}, s32[]{:S(2)}) async-start(s8[12582912]{0:T(1024)(128)(4,1)} %bitcast.163), calls=%async_computation.5 | async-start | bytes 8388608
  429.5 13.1 %slice-start.1 = ((s8[12582912]{0:T(1024)(128)(4,1)}), s8[4194304]{0:T(1024)(128)(4,1)S(1)}, s32[]{:S(2)}) async-start(s8[12582912]{0:T(1024)(128)(4,1)} %bitcast.163), calls=%async_computation.6 | async-start | bytes 8388608
  429.6 13.1 %slice-start.2 = ((s8[12582912]{0:T(1024)(128)(4,1)}), s8[4194304]{0:T(1024)(128)(4,1)S(1)}, s32[]{:S(2)}) async-start(s8[12582912]{0:T(1024)(128)(4,1)} %bitcast.163), calls=%async_computation.7 | async-start | bytes 8388608
  442.7 7.2 copy-start.23
  467.0 6.7 copy-start.11
  467.0 6.7 copy-start.36
  477.0 7.2 slice-start.5
  (60 other events, 206.7 us)
Sparse Core Ops, SparseCore 0:
  487.8 263.9 all-reduce.2
where the time goes:
time: 783 us; the launch traced here: 772 us
  waiting for transfers between devices  365 us (47%)
  matrix products  178 us (23%)
  local copies, waits for them, and re-layouts  139 us (18%)
  other arithmetic  36.9 us (5%)
  blocking collectives  22.5 us (3%)
  between operations  15.6 us (2%)
  starting transfers between devices  15 us (2%)
    psum x1, waiting for transfers between devices, local(): lax.psum((grad_ada, grad_spatial_qkv, grad_spatial_out, grad_temporal_qkv...  258 us
    all_to_all x1, waiting for transfers between devices, local(): lax.all_to_all(qkv_second, 'frame', split_axis=2, concat_axis=1, tiled=True)  54.1 us
    dot_general x7, matrix products, weight_grad(): jnp.einsum('ti,tj->ij', left.reshape(-1, width_in), grad.reshape(-1, widt...  36.4 us
    dot_general x7, matrix products, matmul(): jnp.einsum('...i,ij->...j', left, right, preferred_element_type=jnp.float32)  33.1 us
    all_to_all x1, waiting for transfers between devices, local(): lax.all_to_all(grad_placed, 'frame', split_axis=1, concat_axis=2, tiled=T...  32.5 us
    dot_general x7, matrix products, matmul_back(): jnp.einsum('...j,ij->...i', grad, right, preferred_element_type=jnp.float32)  29.7 us
    dot_general x2, matrix products, attention_backward(): jnp.einsum(forms[0], grad_heads, split_heads(values), preferred_element_t...  27.9 us
    unnamed x176, local copies, waits for them, and re-layouts  26.4 us
  transfers between devices with their start and end apart: 4, of which 4 were waited for; matrix products, arithmetic and copies ran while one was open for 4% of the time, Pallas kernels for 0%

commit v1 on v0

v1 whole, which is shorter than its diff:
```python
import functools

import jax
import jax.numpy as jnp
from jax import lax
from jax.experimental import pallas as pl
from jax.experimental.pallas import tpu as pltpu
from jax.sharding import PartitionSpec as P

D = 384
HEADS = 6
HD = 64
MLP = 1536
F32 = jnp.float32
BF16 = jnp.bfloat16
CHUNKS = 2
GROUP = 16
VMEM = 58 * 2**20


def nn(a, b):
    return lax.dot_general(a, b, (((1,), (0,)), ((), ())), preferred_element_type=F32)


def nt(a, b):
    return lax.dot_general(a, b, (((1,), (1,)), ((), ())), preferred_element_type=F32)


def tn(a, b):
    return lax.dot_general(a, b, (((0,), (0,)), ((), ())), preferred_element_type=F32)


def norm_stats(x):
    c = x - jnp.mean(x, -1, keepdims=True)
    r = lax.rsqrt(jnp.mean(c * c, -1, keepdims=True) + 1e-6)
    return c * r, r


def norm_back(h, n, r):
    return r * (h - jnp.mean(h, -1, keepdims=True) - n * jnp.mean(h * n, -1, keepdims=True))


def spatial_fwd(idx, tok, mod, w_t, wo, qkv_o, mix_o, br_o, tot_o, *rest):
    slots, scr = rest[:-1], rest[-1]
    rows = slots[0].shape[2]
    x = tok[0, 0].astype(F32)
    n, _ = norm_stats(x)
    md = mod[0, 0]
    first = (n * (1.0 + md[1:2]) + md[0:1]).astype(BF16)
    qkv_o[0, 0] = nt(w_t[...], first).astype(BF16)
    for h in range(HEADS):
        a = h * HD
        q = qkv_o[0, 0, a : a + HD] * BF16(0.125)
        k = qkv_o[0, 0, D + a : D + a + HD]
        v = qkv_o[0, 0, 2 * D + a : 2 * D + a + HD]
        s = tn(k, q)
        mx = jnp.max(s, axis=0, keepdims=True)
        p = jnp.exp(s - mx)
        total = jnp.sum(p, axis=0, keepdims=True)
        o = nn(v, p.astype(BF16)) * (1.0 / total)
        tot_o[0, 0, h : h + 1] = mx + jnp.log(total)
        mix_o[0, 0, a : a + HD] = o.astype(BF16)
    br = tn(mix_o[0, 0], wo[...])
    br_o[0, 0] = br.astype(BF16)
    scr[...] = (x + md[2:3] * br).astype(BF16)
    i = idx[0]
    for k, slot in enumerate(slots):
        slot[0, 0] = scr[pl.ds(pl.multiple_of((i ^ k) * rows, GROUP), rows), :]


def call_spatial_fwd(idx, tok, mod, w_t, wo, start, count, n):
    f = tok.shape[1]
    p = tok.shape[2]
    whole = lambda *s: pl.BlockSpec((1, 1) + s, lambda b, f, i: (b + start, f) + (0,) * len(s))
    part = lambda *s: pl.BlockSpec((1, 1) + s, lambda b, f, i: (b, f) + (0,) * len(s))
    fixed = lambda *s: pl.BlockSpec(s, lambda b, f, i: (0,) * len(s))
    sd = lambda s, d: jax.ShapeDtypeStruct((count, f) + s, d)
    return pl.pallas_call(
        spatial_fwd,
        grid_spec=pltpu.PrefetchScalarGridSpec(
            num_scalar_prefetch=1,
            grid=(count, f),
            in_specs=[whole(p, D), whole(3, D), fixed(3 * D, D), fixed(D, D)],
            out_specs=[part(3 * D, p), part(D, p), part(p, D), part(HEADS, p)]
            + [part(p // n, D)] * n,
            scratch_shapes=[pltpu.VMEM((p, D), BF16)],
        ),
        out_shape=[sd((3 * D, p), BF16), sd((D, p), BF16), sd((p, D), BF16), sd((HEADS, p), F32)]
        + [sd((p // n, D), BF16)] * n,
        compiler_params=pltpu.CompilerParams(vmem_limit_bytes=VMEM),
        name="spatial_fwd",
    )(idx, tok, mod, w_t, wo)


def gather_tile(refs, groups):
    f = refs[0].shape[1]
    return jnp.concatenate(
        [
            r[0, j, g * GROUP : (g + 1) * GROUP, :]
            for g in range(groups)
            for r in refs
            for j in range(f)
        ],
        axis=0,
    )


def scatter_tile(refs, value, groups):
    f = refs[0].shape[1]
    at = 0
    for g in range(groups):
        for r in refs:
            for j in range(f):
                r[0, j, g * GROUP : (g + 1) * GROUP, :] = value[at : at + GROUP]
                at += GROUP


def middle(n, first_chunk, *refs):
    refs = list(refs)
    a1, refs = refs[:n], refs[n:]
    ct, refs = refs[:n], refs[n:]
    mod, bias, tq_t, tq, to, up, down = refs[:7]
    refs = refs[7:]
    if not first_chunk:
        inits, refs = refs[:3], refs[3:]
    dl, refs = refs[:n], refs[n:]
    ou, refs = refs[:n], refs[n:]
    gsum, acc_up, acc_down, acc_t = refs[:4]
    qkv_s, p_s, mix_s, dg_s, hid_s, dqkv_s = refs[4:]
    groups = a1[0].shape[2] // GROUP
    frames = n * a1[0].shape[1]
    span = frames * GROUP
    tokens = span * groups

    @pl.when(pl.program_id(0) == 0)
    def _():
        if first_chunk:
            acc_up[...] = jnp.zeros_like(acc_up)
            acc_down[...] = jnp.zeros_like(acc_down)
            acc_t[...] = jnp.zeros_like(acc_t)
        else:
            acc_up[...] = inits[0][...]
            acc_down[...] = inits[1][...]
            acc_t[...] = inits[2][...]

    def per_frame(piece, plus=0.0):
        m = mod[0, :, piece : piece + 1, :] + plus
        return jnp.broadcast_to(m[None], (groups, frames, GROUP, D)).reshape(tokens, D)

    def frame_sum(v):
        return jnp.sum(jnp.sum(v.reshape(groups, frames, GROUP, D), axis=0), axis=1)

    x1 = gather_tile(a1, groups).astype(F32)
    n2, r2 = norm_stats(x1)
    second = (n2 * per_frame(1, 1.0) + per_frame(0)).astype(BF16)
    qkv_s[...] = nt(tq_t[...], second).astype(BF16)
    for g in range(groups):
        cols = slice(g * span, (g + 1) * span)
        for h in range(HEADS):
            a = h * HD
            q = qkv_s[a : a + HD, cols] * BF16(0.125)
            k = qkv_s[D + a : D + a + HD, cols]
            v = qkv_s[2 * D + a : 2 * D + a + HD, cols]
            s = tn(k, q) + bias[0]
            p = jnp.exp(s - jnp.max(s, axis=0, keepdims=True))
            p = p * (1.0 / jnp.sum(p, axis=0, keepdims=True))
            p_s[g * HEADS + h] = p
            mix_s[a : a + HD, cols] = nn(v, p.astype(BF16)).astype(BF16)
    br2 = tn(mix_s[...], to[...])
    x2 = x1 + per_frame(2) * br2
    n3, r3 = norm_stats(x2)
    third = (n3 * per_frame(4, 1.0) + per_frame(3)).astype(BF16)
    step = 256
    br3 = jnp.zeros((tokens, D), F32)
    for c in range(0, MLP, step):
        pre = nn(third, up[:, c : c + step])
        sq = pre * pre
        t = jnp.tanh(pre * (0.7978845608028654 + (0.7978845608028654 * 0.044715) * sq))
        half = 0.5 + 0.5 * t
        hid = (pre * half).astype(BF16)
        hid_s[:, c : c + step] = hid
        inner = 0.7978845608028654 + (3 * 0.7978845608028654 * 0.044715) * sq
        dg_s[:, c : c + step] = half + 0.5 * pre * (1.0 - t * t) * inner
        br3 += nn(hid, down[c : c + step, :])
    gate3 = per_frame(5)
    scatter_tile(ou, (x2 + gate3 * br3).astype(BF16), groups)
    cot = gather_tile(ct, groups).astype(F32)
    gsum[0, :, 5] = frame_sum(cot * br3)
    gb3 = (gate3 * cot).astype(BF16)
    gb3_t = gb3.T
    third_t = third.T
    g3 = jnp.zeros((tokens, D), F32)
    for c in range(0, MLP, step):
        acc_down[:, c : c + step] += nn(gb3_t, hid_s[:, c : c + step])
        gp = (nt(gb3, down[c : c + step, :]) * dg_s[:, c : c + step]).astype(BF16)
        acc_up[:, c : c + step] += nn(third_t, gp)
        g3 += nt(gp, up[:, c : c + step])
    gsum[0, :, 3] = frame_sum(g3)
    gsum[0, :, 4] = frame_sum(g3 * n3)
    dx3 = norm_back(g3 * per_frame(4, 1.0), n3, r3)
    ga2 = cot + dx3
    gsum[0, :, 2] = frame_sum(ga2 * br2)
    gb2 = (per_frame(2) * ga2).astype(BF16)
    acc_t[:, 3 * D :] += nn(mix_s[...], gb2)
    gm_t = nt(to[...], gb2).astype(BF16)
    for g in range(groups):
        cols = slice(g * span, (g + 1) * span)
        for h in range(HEADS):
            a = h * HD
            q = qkv_s[a : a + HD, cols] * BF16(0.125)
            k = qkv_s[D + a : D + a + HD, cols]
            v = qkv_s[2 * D + a : 2 * D + a + HD, cols]
            go = gm_t[a : a + HD, cols]
            p = p_s[g * HEADS + h]
            dp = tn(v, go)
            ds = (p * (dp - jnp.sum(p * dp, axis=0, keepdims=True))).astype(BF16)
            dqkv_s[2 * D + a : 2 * D + a + HD, cols] = nt(go, p.astype(BF16)).astype(BF16)
            dqkv_s[D + a : D + a + HD, cols] = nt(q, ds).astype(BF16)
            dqkv_s[a : a + HD, cols] = (nn(k, ds) * 0.125).astype(BF16)
    dqkv = dqkv_s[...]
    acc_t[:, : 3 * D] += nt(second.T, dqkv)
    g2 = nn(tq[...], dqkv).T
    gsum[0, :, 0] = frame_sum(g2)
    gsum[0, :, 1] = frame_sum(g2 * n2)
    dx2 = norm_back(g2 * per_frame(1, 1.0), n2, r2)
    scatter_tile(dl, (dx3 + dx2).astype(BF16), groups)


def call_middle(a1, ct, mod, bias, tq_t, tq, to, up, down, inits, start):
    n = len(a1)
    count, f, rows = a1[0].shape[:3]
    frames = n * f
    span = frames * GROUP
    tokens = frames * rows
    groups = rows // GROUP
    part = lambda *s: pl.BlockSpec((1,) + s, lambda b: (b,) + (0,) * len(s))
    whole = lambda *s: pl.BlockSpec((1,) + s, lambda b: (b + start,) + (0,) * len(s))
    fixed = lambda *s: pl.BlockSpec(s, lambda b: (0,) * len(s), pipeline_mode=pl.Buffered(1))
    accs = [(D, MLP)] * 3
    sd = jax.ShapeDtypeStruct
    return pl.pallas_call(
        functools.partial(middle, n, not inits),
        grid=(count,),
        in_specs=[part(f, rows, D)] * n
        + [whole(f, rows, D)] * n
        + [whole(frames, 6, D), whole(span, span), fixed(3 * D, D), fixed(D, 3 * D)]
        + [fixed(D, D), fixed(D, MLP), fixed(MLP, D)]
        + [fixed(*s) for s in accs[: len(inits)]],
        out_specs=[part(f, rows, D)] * (2 * n)
        + [part(frames, 6, D)]
        + [pl.BlockSpec(s, lambda b: (0, 0)) for s in accs],
        out_shape=[sd((count, f, rows, D), BF16)] * (2 * n)
        + [sd((count, frames, 6, D), F32)]
        + [sd(s, F32) for s in accs],
        scratch_shapes=[
            pltpu.VMEM((3 * D, tokens), BF16),
            pltpu.VMEM((groups * HEADS, span, span), F32),
            pltpu.VMEM((D, tokens), BF16),
            pltpu.VMEM((tokens, MLP), F32),
            pltpu.VMEM((tokens, MLP), BF16),
            pltpu.VMEM((3 * D, tokens), BF16),
        ],
        compiler_params=pltpu.CompilerParams(vmem_limit_bytes=VMEM),
        name="middle",
    )(*a1, *ct, mod, bias, tq_t, tq, to, up, down, *inits)


def spatial_bwd(n, first_chunk, idx, tok, cot, mod, qkv, mix, br, tot, wo, *rest):
    rest = list(rest)
    if not first_chunk:
        init, rest = rest[0], rest[1:]
    dl, rest = rest[:n], rest[n:]
    dqkv_o, ga_o, gg_o, acc, scr = rest

    @pl.when((pl.program_id(0) == 0) & (pl.program_id(1) == 0))
    def _():
        acc[...] = jnp.zeros_like(acc) if first_chunk else init[...]

    rows = dl[0].shape[2]
    i = idx[0]
    for k in range(n):
        scr[pl.ds(pl.multiple_of((i ^ k) * rows, GROUP), rows), :] = dl[k][0, 0]
    ga = cot[0, 0].astype(F32) + scr[...].astype(F32)
    ga_o[0, 0] = ga
    md = mod[0, 0]
    gg_o[0, 0] = jnp.sum(ga * br[0, 0].astype(F32), axis=0, keepdims=True)
    gb = (md[2:3] * ga).astype(BF16)
    acc[:, 3 * D :] += nn(mix[0, 0], gb)
    gm = nt(wo[...], gb).astype(BF16)
    for h in range(HEADS):
        a = h * HD
        q = qkv[0, 0, a : a + HD] * BF16(0.125)
        k = qkv[0, 0, D + a : D + a + HD]
        v = qkv[0, 0, 2 * D + a : 2 * D + a + HD]
        go = gm[a : a + HD]
        p = jnp.exp(tn(k, q) - tot[0, 0, h : h + 1])
        dp = tn(v, go)
        ds = (p * (dp - jnp.sum(p * dp, axis=0, keepdims=True))).astype(BF16)
        dqkv_o[0, 0, 2 * D + a : 2 * D + a + HD] = nt(go, p.astype(BF16)).astype(BF16)
        dqkv_o[0, 0, D + a : D + a + HD] = nt(q, ds).astype(BF16)
        dqkv_o[0, 0, a : a + HD] = (nn(k, ds) * 0.125).astype(BF16)
    nrm, _ = norm_stats(tok[0, 0].astype(F32))
    first = (nrm * (1.0 + md[1:2]) + md[0:1]).astype(BF16)
    acc[:, : 3 * D] += nt(first.T, dqkv_o[0, 0])


def call_spatial_bwd(idx, tok, cot, mod, qkv, mix, br, tot, wo, init, dl, start):
    n = len(dl)
    count, f, rows = dl[0].shape[:3]
    p = tok.shape[2]
    whole = lambda *s: pl.BlockSpec((1, 1) + s, lambda b, f, i: (b + start, f) + (0,) * len(s))
    part = lambda *s: pl.BlockSpec((1, 1) + s, lambda b, f, i: (b, f) + (0,) * len(s))
    fixed = lambda *s: pl.BlockSpec(s, lambda b, f, i: (0,) * len(s), pipeline_mode=pl.Buffered(1))
    sd = lambda s, d: jax.ShapeDtypeStruct((count, f) + s, d)
    return pl.pallas_call(
        functools.partial(spatial_bwd, n, not init),
        grid_spec=pltpu.PrefetchScalarGridSpec(
            num_scalar_prefetch=1,
            grid=(count, f),
            in_specs=[whole(p, D), whole(p, D), whole(3, D), part(3 * D, p), part(D, p)]
            + [part(p, D), part(HEADS, p), fixed(D, D)]
            + [fixed(D, MLP)] * len(init)
            + [part(rows, D)] * n,
            out_specs=[part(3 * D, p), part(p, D), part(1, D)]
            + [pl.BlockSpec((D, MLP), lambda b, f, i: (0, 0))],
            scratch_shapes=[pltpu.VMEM((p, D), BF16)],
        ),
        out_shape=[sd((3 * D, p), BF16), sd((p, D), F32), sd((1, D), F32)]
        + [jax.ShapeDtypeStruct((D, MLP), F32)],
        compiler_params=pltpu.CompilerParams(vmem_limit_bytes=VMEM),
        name="spatial_bwd",
    )(idx, tok, cot, mod, qkv, mix, br, tot, wo, *init, *dl)


def last_step(n, idx, tok, mod, w_t, dqkv, ga, *rest):
    ou, rest = rest[:n], rest[n:]
    grad_o, out_o, gs_o = rest
    rows = ou[0].shape[2]
    i = idx[0]
    for k in range(n):
        out_o[0, 0, pl.ds(pl.multiple_of((i ^ k) * rows, GROUP), rows), :] = ou[k][0, 0]
    g = tn(dqkv[0, 0], w_t[...])
    nrm, r = norm_stats(tok[0, 0].astype(F32))
    md = mod[0, 0]
    gs_o[0, 0, 0:1] = jnp.sum(g, axis=0, keepdims=True)
    gs_o[0, 0, 1:2] = jnp.sum(g * nrm, axis=0, keepdims=True)
    grad_o[0, 0] = ga[0, 0] + norm_back(g * (1.0 + md[1:2]), nrm, r)


def call_last(idx, tok, mod, w_t, dqkv, ga, ou, start):
    n = len(ou)
    count, f, rows = ou[0].shape[:3]
    p = tok.shape[2]
    whole = lambda *s: pl.BlockSpec((1, 1) + s, lambda b, f, i: (b + start, f) + (0,) * len(s))
    part = lambda *s: pl.BlockSpec((1, 1) + s, lambda b, f, i: (b, f) + (0,) * len(s))
    fixed = lambda *s: pl.BlockSpec(s, lambda b, f, i: (0,) * len(s), pipeline_mode=pl.Buffered(1))
    sd = lambda s, d: jax.ShapeDtypeStruct((count, f) + s, d)
    return pl.pallas_call(
        functools.partial(last_step, n),
        grid_spec=pltpu.PrefetchScalarGridSpec(
            num_scalar_prefetch=1,
            grid=(count, f),
            in_specs=[whole(p, D), whole(3, D), fixed(3 * D, D), part(3 * D, p), part(p, D)]
            + [part(rows, D)] * n,
            out_specs=[part(p, D), part(p, D), part(2, D)],
        ),
        out_shape=[sd((p, D), F32), sd((p, D), BF16), sd((2, D), F32)],
        compiler_params=pltpu.CompilerParams(vmem_limit_bytes=VMEM),
        name="last_step",
    )(idx, tok, mod, w_t, dqkv, ga, *ou)


def swap(x, axis, mask):
    size = lax.axis_size(axis)
    return lax.ppermute(x, axis, [(s, s ^ mask) for s in range(size)])


def bits_of(axis):
    return [(axis, b) for b in range(lax.axis_size(axis).bit_length() - 1)]


def bit_of(axis, b):
    return (lax.axis_index(axis) >> b) & 1


def reduce_all(g):
    frame, pack = bits_of("frame"), bits_of("pack")
    steps = frame[:1] + pack + frame[1:]
    halved = []
    for axis, b in steps:
        rows = g.shape[0]
        if rows % 32 == 0:
            mine = bit_of(axis, b)
            half = rows // 2
            send = lax.dynamic_slice_in_dim(g, (1 - mine) * half, half, 0).astype(BF16)
            keep = lax.dynamic_slice_in_dim(g, mine * half, half, 0)
            g = keep.astype(F32) + swap(send, axis, 1 << b).astype(F32)
            halved.append((axis, b))
        else:
            send = g.astype(BF16)
            g = send.astype(F32) + swap(send, axis, 1 << b).astype(F32)
    g = g.astype(BF16)
    return spread(g, halved[::-1])


def spread(g, steps):
    for axis, b in steps:
        other = swap(g, axis, 1 << b)
        mine = bit_of(axis, b) == 1
        g = jnp.concatenate([jnp.where(mine, other, g), jnp.where(mine, g, other)], axis=0)
    return g


def local(
    tokens,
    condition,
    clip_lengths,
    ada_weight,
    spatial_qkv,
    spatial_out,
    temporal_qkv,
    temporal_out,
    mlp_up,
    mlp_down,
    cotangent,
):
    n = lax.axis_size("frame")
    i = lax.axis_index("frame")
    idx = i.reshape(1).astype(jnp.int32)
    packs, f, patches = tokens.shape[:3]
    rows = patches // n
    count = packs // CHUNKS
    every = bits_of("frame") + bits_of("pack")

    cut = lambda v, k: lax.dynamic_slice_in_dim(v, (i ^ k) * rows, rows, 2)
    send = lambda parts: [parts[0]] + [swap(parts[k], "frame", k) for k in range(1, n)]

    silu = lambda v: v / (1.0 + jnp.exp(-v))
    cond_slots = send([condition] * n)
    activated = silu(condition.astype(F32)).astype(BF16)
    act_slots = silu(jnp.stack(cond_slots, 1).astype(F32)).astype(BF16)
    dot = functools.partial(jnp.einsum, preferred_element_type=F32)
    mod_own = dot("bfi,ij->bfj", activated, ada_weight[:, : 3 * D]).reshape(packs, f, 3, D)
    mod_all = dot("bkfi,ij->bkfj", act_slots, ada_weight[:, 3 * D :])
    mod_all = mod_all.reshape(packs, n * f, 6, D)

    frame_ids = jnp.concatenate([(i ^ k) * f + jnp.arange(f, dtype=jnp.int32) for k in range(n)])
    width = clip_lengths.shape[1]
    ends = [jnp.sum(clip_lengths[:, : j + 1], axis=1) for j in range(width)]
    segment = sum((e[:, None] <= frame_ids[None, :]).astype(jnp.int32) for e in ends)
    segment = jnp.repeat(segment, GROUP, axis=1)
    patch = jnp.tile(jnp.arange(GROUP, dtype=jnp.int32), n * f)
    allowed = (segment[:, :, None] == segment[:, None, :]) & (patch[:, None] == patch[None, :])
    bias = jnp.where(allowed, 0.0, -1e30).astype(F32)

    sq_t = spatial_qkv.T
    tq_t = temporal_qkv.T
    ct = send([cut(cotangent, k) for k in range(n)])

    fwd = []
    for c in range(CHUNKS):
        res = call_spatial_fwd(idx, tokens, mod_own, sq_t, spatial_out, c * count, count, n)
        fwd.append((res[:4], send(list(res[4:]))))

    accs, mids = [], []
    for c in range(CHUNKS):
        res = call_middle(
            fwd[c][1], ct, mod_all, bias, tq_t, temporal_qkv, temporal_out, mlp_up, mlp_down,
            accs, c * count,
        )
        accs = list(res[2 * n + 1 :])
        sums = res[2 * n].reshape(count, n, f, 6, D)
        mids.append((send(list(res[:n])), send(list(res[n : 2 * n])), send([sums[:, k] for k in range(n)])))
    early = reduce_all(jnp.concatenate(accs, axis=0))

    acc, backs = [], []
    for c in range(CHUNKS):
        qkv, mix, br, tot = fwd[c][0]
        res = call_spatial_bwd(
            idx, tokens, cotangent, mod_own, qkv, mix, br, tot, spatial_out, acc, mids[c][0],
            c * count,
        )
        acc = [res[3]]
        backs.append(res)
    late = reduce_all(acc[0])

    lasts = []
    for c in range(CHUNKS):
        dqkv, ga, gate_sum, _ = backs[c]
        lasts.append(call_last(idx, tokens, mod_own, sq_t, dqkv, ga, mids[c][1], c * count))
    grad_tokens = jnp.concatenate([v[0] for v in lasts], 0)
    output = jnp.concatenate([v[1] for v in lasts], 0)

    grad_mod = jnp.concatenate(
        [
            jnp.concatenate([lasts[c][2], backs[c][2], sum(mids[c][2])], axis=2)
            for c in range(CHUNKS)
        ],
        axis=0,
    ).astype(BF16)
    grad_mod = grad_mod.reshape(packs * f, 9 * D)
    all_act = spread(activated.reshape(packs * f, D), every)
    all_mod = spread(grad_mod, every)
    grad_ada = dot("ti,tj->ij", all_act, all_mod)
    back = dot("tj,ij->ti", grad_mod, ada_weight).reshape(packs, f, D)
    cf = condition.astype(F32)
    sig = 1.0 / (1.0 + jnp.exp(-cf))
    grad_condition = back * (sig * (1.0 + cf * (1.0 - sig)))

    early = early.astype(F32)
    late = late.astype(F32)
    return (
        output,
        grad_tokens,
        grad_condition,
        grad_ada,
        late[:, : 3 * D],
        late[:, 3 * D :],
        early[2 * D :, : 3 * D],
        early[2 * D :, 3 * D :],
        early[:D],
        early[D : 2 * D].T,
    )


def solution(mesh):
    tok = P("pack", "frame", None, None)
    cond = P("pack", "frame", None)
    return jax.shard_map(
        local,
        mesh=mesh,
        in_specs=(tok, cond, P("pack", None), P(), P(), P(), P(), P(), P(), P(), tok),
        out_specs=(tok, tok, cond, P(), P(), P(), P(), P(), P(), P()),
        check_vma=False,
    )
```

time: 783 us -> 410 us (0.52)
  waiting for transfers between devices: 365 us -> 143 us
  matrix products: 178 us -> 9.81 us
  Pallas kernels: 0 us -> 163 us
  local copies, waits for them, and re-layouts: 139 us -> 25.4 us
  starting transfers between devices: 15 us -> 45.1 us
  blocking collectives: 22.5 us -> 0 us
  other arithmetic: 36.9 us -> 15.4 us
  between operations: 15.6 us -> 2.08 us
    psum x1 -> x0, waiting for transfers between devices: 258 us -> none  [local(): lax.psum((grad_ada, grad_spatial_qkv, grad_spatial_out, grad_temporal_qkv...]
    dot_general x33 -> x4, matrix products: 178 us -> 9.81 us  [the longest x1 3.28 us: local(): grad_ada = dot('ti,tj->ij', all_act, all_mod)]
    pallas_call x0 -> x8, Pallas kernels: none -> 163 us  [the longest x2 93.6 us: call_middle(): pl.pallas_call(functools.partial(middle, n, not inits), grid=(count,), in...]
    ppermute x0 -> x56, waiting for transfers between devices: none -> 143 us  [swap(): return lax.ppermute(x, axis, [(s, s ^ mask) for s in range(size)])]
    all_to_all x3 -> x0, waiting for transfers between devices: 107 us -> none  [the longest x1 54.1 us: local(): lax.all_to_all(qkv_second, 'frame', split_axis=2, concat_axis=1, tiled=True)]
    reshape x10 -> x3, local copies, waits for them, and re-layouts: 49.8 us -> 1.67 us  [the longest x1 1 us: local(): mod_all = mod_all.reshape(packs, n * f, 6, D)]
    ppermute x0 -> x56, starting transfers between devices: none -> 45.1 us  [swap(): return lax.ppermute(x, axis, [(s, s ^ mask) for s in range(size)])]
    all_to_all x1 -> x0, blocking collectives: 22.5 us -> none  [local(): lax.all_to_all(grad_mixed_second, 'frame', split_axis=2, concat_axis=1, t...]
  transfers between devices with their start and end apart: 4 -> 56, of which waited for: 4 -> 20; matrix products, arithmetic and copies ran while one was open for 4% -> 9% of each run, Pallas kernels for 0% -> 40%
where the time goes in v1:
time: 410 us; the launch traced here: 403 us
  Pallas kernels  163 us (40%)
  waiting for transfers between devices  143 us (35%)
  starting transfers between devices  45.1 us (11%)
  local copies, waits for them, and re-layouts  25.4 us (6%)
  other arithmetic  15.4 us (4%)
  matrix products  9.81 us (2%)
    ppermute x56, waiting for transfers between devices, swap(): return lax.ppermute(x, axis, [(s, s ^ mask) for s in range(size)])  143 us
    pallas_call x2, Pallas kernels, call_middle(): pl.pallas_call(functools.partial(middle, n, not inits), grid=(count,), in...  93.6 us
    ppermute x56, starting transfers between devices, swap(): return lax.ppermute(x, axis, [(s, s ^ mask) for s in range(size)])  45.1 us
    pallas_call x2, Pallas kernels, call_spatial_bwd(): pl.pallas_call(functools.partial(spatial_bwd, n, not init), grid_spec=plt...  29.3 us
    pallas_call x2, Pallas kernels, call_spatial_fwd(): pl.pallas_call(spatial_fwd, grid_spec=pltpu.PrefetchScalarGridSpec(num_sc...  26.7 us
    unnamed x104, local copies, waits for them, and re-layouts  13.4 us
    pallas_call x2, Pallas kernels, call_last(): pl.pallas_call(functools.partial(last_step, n), grid_spec=pltpu.PrefetchS...  13.1 us
  transfers between devices with their start and end apart: 56, of which 20 were waited for; matrix products, arithmetic and copies ran while one was open for 9% of the time, Pallas kernels for 40%

profile of v1, /device:TPU:0, one launch (start us, length us, event | category | flops | bytes accessed | tf_op | source)
XLA Modules:
  0.0 403.3 jit_solution(6735518240523561984)
XLA Ops:
  11.8 7.3 %collective-permute-done.31 = bf16[16,384]{1,0:T(8,128)(2,1)S(1)} collective-permute-done((bf16[16,384]{1,0:T(8,128)(2,1)S(1)}, bf16[16,384]{1,0:T(8,128)(2,1)S(1)}, u32[]{:S(2)}, u32[]{:S(2)}) %collective-permute-start.31) | collective-permute-done | bytes 12320 | tf_op jit(solution)/shard_map/ppermute | solution.py:375
  23.7 13.3 %spatial_fwd.3 = (bf16[2,2,1152,256]{3,2,1,0:T(8,128)(2,1)}, bf16[2,2,384,256]{3,2,1,0:T(8,128)(2,1)}, bf16[2,2,256,384]{3,2,1,0:T(8,128)(2,1)}, f32[2,2,6,256]{...) custom-call(s32[1]{0:T(128)} %bitcast.idx, ...), custom_call_target="tpu_custom_call" | custom-call | tf_op jit(solution)/shard_map/spatial_fwd/pallas_call | solution.py:78
  37.0 13.4 %spatial_fwd.2 = (bf16[2,2,1152,256]{3,2,1,0:T(8,128)(2,1)}, bf16[2,2,384,256]{3,2,1,0:T(8,128)(2,1)}, bf16[2,2,256,384]{3,2,1,0:T(8,128)(2,1)}, f32[2,2,6,256]{...) custom-call(s32[1]{0:T(128)} %bitcast.idx, ...), custom_call_target="tpu_custom_call" | custom-call | tf_op jit(solution)/shard_map/spatial_fwd/pallas_call | solution.py:78
  66.5 6.7 %collective-permute-done.1.refs_2_ = bf16[2,2,64,384]{3,2,1,0:T(8,128)(2,1)S(1)} collective-permute-done((bf16[2,2,64,384]{3,2,1,0:T(8,128)(2,1)}, bf16[2,2,64,384]{3,2,1,0:T(8,128)(2,1)S(1)}, u32[]{:S(2)}, u32[]{:S(2)}) %collective-permute-start.1) | collective-permute-done | bytes 196640 | tf_op jit(solution)/shard_map/ppermute | solution.py:375
  77.4 46.0 %middle.2 = (bf16[2,2,64,384]{3,2,1,0:T(8,128)(2,1)}, bf16[2,2,64,384]{3,2,1,0:T(8,128)(2,1)}, bf16[2,2,64,384]{3,2,1,0:T(8,128)(2,1)}, bf16[2,2,64,384]{3,2,1,0...) custom-call(bf16[2,2,64,384]{3,2,1,0:T(8,128)(2,1)} %get-tuple-eleme, ...), custom_call_target="tpu_custom_call" | custom-call | tf_op jit(solution)/shard_map/middle/pallas_call | solution.py:241
  127.2 47.6 %middle.3 = (bf16[2,2,64,384]{3,2,1,0:T(8,128)(2,1)}, bf16[2,2,64,384]{3,2,1,0:T(8,128)(2,1)}, bf16[2,2,64,384]{3,2,1,0:T(8,128)(2,1)}, bf16[2,2,64,384]{3,2,1,0...) custom-call(bf16[2,2,64,384]{3,2,1,0:T(8,128)(2,1)} %get-tuple-eleme, ...), custom_call_target="tpu_custom_call" | custom-call | tf_op jit(solution)/shard_map/middle/pallas_call | solution.py:241
  191.2 3.0 collective-permute-done.13.rest_2_
  194.2 3.7 collective-permute-done.14.rest_3_
  199.6 14.2 %spatial_bwd.2 = (bf16[2,2,1152,256]{3,2,1,0:T(8,128)(2,1)}, f32[2,2,256,384]{3,2,1,0:T(8,128)}, f32[2,2,1,384]{3,2,1,0:T(1,128)}, f32[384,1536]{1,0:T(8,128)}) custom-call(s32[1]{0:T(128)} %bitcast.idx, bf16[4,2,256,384]{3,2,1,0:T(8,128)(2,1)} %tok.11, bf16[4,2,256,384]{3,2,1,0:T(8,128)(2,1)} %cot.3, f32[4,2,3,384]{3,2,1,0:T(4,128)} %reshape.87.mod, ...), custom_call_target="tpu_custom_call" | custom-call | tf_op jit(solution)/shard_map/spatial_bwd/pallas_call | solution.py:315
  213.9 6.4 %last_step.2 = (f32[2,2,256,384]{3,2,1,0:T(8,128)}, bf16[2,2,256,384]{3,2,1,0:T(8,128)(2,1)}, f32[2,2,2,384]{3,2,1,0:T(2,128)}) custom-call(s32[1]{0:T(128)} %bitcast.idx, bf16[4,2,256,384]{3,2,1,0:T(8,128)(2,1)} %tok.11, f32[4,2,3,384]{3,2,1,0:T(4,128)} %reshape.87.mod, bf16[1152,384]{1,0:T(8,128)(2,1)} %bitcast.74, ...), custom_call_target="tpu_custom_call" | custom-call | tf_op jit(solution)/shard_map/last_step/pallas_call | solution.py:358
  221.6 15.1 %spatial_bwd.3 = (bf16[2,2,1152,256]{3,2,1,0:T(8,128)(2,1)}, f32[2,2,256,384]{3,2,1,0:T(8,128)}, f32[2,2,1,384]{3,2,1,0:T(1,128)}, f32[384,1536]{1,0:T(8,128)}) custom-call(s32[1]{0:T(128)} %bitcast.idx, bf16[4,2,256,384]{3,2,1,0:T(8,128)(2,1)} %tok.11, bf16[4,2,256,384]{3,2,1,0:T(8,128)(2,1)} %cot.3, f32[4,2,3,384]{3,2,1,0:T(4,128)} %reshape.87.mod, ...), custom_call_target="tpu_custom_call" | custom-call | tf_op jit(solution)/shard_map/spatial_bwd/pallas_call | solution.py:315
  237.5 6.7 %last_step.3 = (f32[2,2,256,384]{3,2,1,0:T(8,128)}, bf16[2,2,256,384]{3,2,1,0:T(8,128)(2,1)}, f32[2,2,2,384]{3,2,1,0:T(2,128)}) custom-call(s32[1]{0:T(128)} %bitcast.idx, bf16[4,2,256,384]{3,2,1,0:T(8,128)(2,1)} %tok.11, f32[4,2,3,384]{3,2,1,0:T(4,128)} %reshape.87.mod, bf16[1152,384]{1,0:T(8,128)(2,1)} %bitcast.75, ...), custom_call_target="tpu_custom_call" | custom-call | tf_op jit(solution)/shard_map/last_step/pallas_call | solution.py:358
  248.3 3.2 fusion.9
  253.1 4.0 %collective-permute-done.36 = bf16[16,3456]{1,0:T(8,128)(2,1)S(1)} collective-permute-done((bf16[16,3456]{1,0:T(8,128)(2,1)S(1)}, bf16[16,3456]{1,0:T(8,128)(2,1)S(1)}, u32[]{:S(2)}, u32[]{:S(2)}) %collective-permute-start.36) | collective-permute-done | bytes 110624 | tf_op jit(solution)/shard_map/ppermute | solution.py:375
  261.3 3.1 collective-permute-done.37
  268.3 7.1 %collective-permute-done.38 = bf16[64,3456]{1,0:T(8,128)(2,1)S(1)} collective-permute-done((bf16[64,3456]{1,0:T(8,128)(2,1)S(1)}, bf16[64,3456]{1,0:T(8,128)(2,1)S(1)}, u32[]{:S(2)}, u32[]{:S(2)}) %collective-permute-start.38) | collective-permute-done | bytes 442400 | tf_op jit(solution)/shard_map/ppermute | solution.py:375
  276.9 14.9 %collective-permute-done.49 = bf16[288,1536]{1,0:T(8,128)(2,1)S(1)} collective-permute-done((bf16[288,1536]{1,0:T(8,128)(2,1)S(1)}, bf16[288,1536]{1,0:T(8,128)(2,1)S(1)}, u32[]{:S(2)}, u32[]{:S(2)}) %collective-permute-start.49) | collective-permute-done | bytes 884768 | tf_op jit(solution)/shard_map/ppermute | solution.py:375
  296.4 8.7 %collective-permute-done.50 = bf16[144,1536]{1,0:T(8,128)(2,1)S(1)} collective-permute-done((bf16[144,1536]{1,0:T(8,128)(2,1)S(1)}, bf16[144,1536]{1,0:T(8,128)(2,1)S(1)}, u32[]{:S(2)}, u32[]{:S(2)}) %collective-permute-start.50) | collective-permute-done | bytes 442400 | tf_op jit(solution)/shard_map/ppermute | solution.py:375
  307.6 19.2 %collective-permute-done.51 = bf16[144,1536]{1,0:T(8,128)(2,1)S(1)} collective-permute-done((bf16[144,1536]{1,0:T(8,128)(2,1)S(1)}, bf16[144,1536]{1,0:T(8,128)(2,1)S(1)}, u32[]{:S(2)}, u32[]{:S(2)}) %collective-permute-start.51) | collective-permute-done | bytes 442400 | tf_op jit(solution)/shard_map/ppermute | solution.py:375
  327.1 11.4 %collective-permute-done.52 = bf16[144,1536]{1,0:T(8,128)(2,1)S(1)} collective-permute-done((bf16[144,1536]{1,0:T(8,128)(2,1)S(1)}, bf16[144,1536]{1,0:T(8,128)(2,1)S(1)}, u32[]{:S(2)}, u32[]{:S(2)}) %collective-permute-start.52) | collective-permute-done | bytes 442400 | tf_op jit(solution)/shard_map/ppermute | solution.py:375
  339.4 9.9 %collective-permute-done.53 = bf16[144,1536]{1,0:T(8,128)(2,1)S(1)} collective-permute-done((bf16[144,1536]{1,0:T(8,128)(2,1)S(1)}, bf16[144,1536]{1,0:T(8,128)(2,1)S(1)}, u32[]{:S(2)}, u32[]{:S(2)}) %collective-permute-start.53) | collective-permute-done | bytes 442400 | tf_op jit(solution)/shard_map/ppermute | solution.py:375
  351.9 16.8 %collective-permute-done.54 = bf16[288,1536]{1,0:T(8,128)(2,1)S(1)} collective-permute-done((bf16[288,1536]{1,0:T(8,128)(2,1)S(1)}, bf16[288,1536]{1,0:T(8,128)(2,1)S(1)}, u32[]{:S(2)}, u32[]{:S(2)}) %collective-permute-start.54) | collective-permute-done | bytes 884768 | tf_op jit(solution)/shard_map/ppermute | solution.py:375
  369.2 19.7 %collective-permute-done.39 = bf16[128,3456]{1,0:T(8,128)(2,1)S(1)} collective-permute-done((bf16[128,3456]{1,0:T(8,128)(2,1)S(1)}, bf16[128,3456]{1,0:T(8,128)(2,1)S(1)}, u32[]{:S(2)}, u32[]{:S(2)}) %collective-permute-start.39) | collective-permute-done | bytes 884768 | tf_op jit(solution)/shard_map/ppermute | solution.py:375
  389.3 3.3 fusion.2
  (290 shorter events, 96.2 us)
Async XLA Ops:
  0.7 51.1 %collective-permute-start.6 = (bf16[4,2,384]{2,1,0:T(2,128)(2,1)}, bf16[4,2,384]{2,1,0:T(2,128)(2,1)S(1)}, u32[]{:S(2)}, u32[]{:S(2)}) collective-permute-start(bf16[4,2,384]{2,1,0:T(2,128)(2,1)} %param.12), channel_id=1, source_target_pairs={{0,8},{8,0},{16,24},{24,16},{1,9},{9,1},{17,25},{25,17},{2,10},{10... | collective-permute-start | bytes 18440 | tf_op jit(solution)/shard_map/ppermute | solution.py:375
  1.2 52.1 %collective-permute-start.8 = (bf16[4,2,384]{2,1,0:T(2,128)(2,1)}, bf16[4,2,384]{2,1,0:T(2,128)(2,1)S(1)}, u32[]{:S(2)}, u32[]{:S(2)}) collective-permute-start(bf16[4,2,384]{2,1,0:T(2,128)(2,1)} %param.12), channel_id=1, source_target_pairs={{0,24},{8,16},{16,8},{24,0},{1,25},{9,17},{17,9},{25,1},{2,26},{10... | collective-permute-start | bytes 18440 | tf_op jit(solution)/shard_map/ppermute | solution.py:375
  3.8 49.6 %collective-permute-start.7 = (bf16[4,2,384]{2,1,0:T(2,128)(2,1)}, bf16[4,2,384]{2,1,0:T(2,128)(2,1)S(1)}, u32[]{:S(2)}, u32[]{:S(2)}) collective-permute-start(bf16[4,2,384]{2,1,0:T(2,128)(2,1)} %param.12), channel_id=1, source_target_pairs={{0,16},{8,24},{16,0},{24,8},{1,17},{9,25},{17,1},{25,9},{2,18},{10... | collective-permute-start | bytes 18440 | tf_op jit(solution)/shard_map/ppermute | solution.py:375
  7.2 67.7 %collective-permute-start.5 = (bf16[4,2,64,384]{3,2,1,0:T(8,128)(2,1)S(1)}, bf16[4,2,64,384]{3,2,1,0:T(8,128)(2,1)S(1)}, u32[]{:S(2)}, u32[]{:S(2)}) collective-permute-start(bf16[4,2,64,384]{3,2,1,0:T(8,128)(2,1)S(1)} %get-tuple-element.166), channel_id=1, source_target_pairs={{0,24},{8,16},{16,8},{24,0},{1,25},{9,17},{17,9},{25,1},{2,26},{10... | collective-permute-start | bytes 1179656 | tf_op jit(solution)/shard_map/ppermute | solution.py:375
  19.2 34.9 %collective-permute-start.32 = (bf16[32,384]{1,0:T(8,128)(2,1)S(1)}, bf16[32,384]{1,0:T(8,128)(2,1)S(1)}, u32[]{:S(2)}, u32[]{:S(2)}) collective-permute-start(bf16[32,384]{1,0:T(8,128)(2,1)S(1)} %pad_maximum_fusion.12), channel_id=1, source_target_pairs={{0,1},{1,0},{2,3},{3,2},{4,5},{5,4},{6,7},{7,6},{8,9},{9,8},{10,11... | collective-permute-start | bytes 73736 | tf_op jit(solution)/shard_map/ppermute | solution.py:375
  51.8 24.7 %collective-permute-start.4 = (bf16[4,2,64,384]{3,2,1,0:T(8,128)(2,1)S(1)}, bf16[4,2,64,384]{3,2,1,0:T(8,128)(2,1)S(1)}, u32[]{:S(2)}, u32[]{:S(2)}) collective-permute-start(bf16[4,2,64,384]{3,2,1,0:T(8,128)(2,1)S(1)} %get-tuple-element.167), channel_id=1, source_target_pairs={{0,16},{8,24},{16,0},{24,8},{1,17},{9,25},{17,1},{25,9},{2,18},{10... | collective-permute-start | bytes 1179656 | tf_op jit(solution)/shard_map/ppermute | solution.py:375
  73.1 51.8 %collective-permute-start.15 = (bf16[2,2,64,384]{3,2,1,0:T(8,128)(2,1)}, bf16[2,2,64,384]{3,2,1,0:T(8,128)(2,1)S(1)}, u32[]{:S(2)}, u32[]{:S(2)}) collective-permute-start(bf16[2,2,64,384]{3,2,1,0:T(8,128)(2,1)} %get-tuple-element.89), channel_id=1, source_target_pairs={{0,8},{8,0},{16,24},{24,16},{1,9},{9,1},{17,25},{25,17},{2,10},{10... | collective-permute-start | bytes 589832 | tf_op jit(solution)/shard_map/ppermute | solution.py:375
  73.4 52.8 %collective-permute-start.16 = (bf16[2,2,64,384]{3,2,1,0:T(8,128)(2,1)S(1)}, bf16[2,2,64,384]{3,2,1,0:T(8,128)(2,1)S(1)}, u32[]{:S(2)}, u32[]{:S(2)}) collective-permute-start(bf16[2,2,64,384]{3,2,1,0:T(8,128)(2,1)S(1)} %copy-done.40), channel_id=1, source_target_pairs={{0,16},{8,24},{16,0},{24,8},{1,17},{9,25},{17,1},{25,9},{2,18},{10... | collective-permute-start | bytes 589832 | tf_op jit(solution)/shard_map/ppermute | solution.py:375
  74.9 51.7 %collective-permute-start.17 = (bf16[2,2,64,384]{3,2,1,0:T(8,128)(2,1)S(1)}, bf16[2,2,64,384]{3,2,1,0:T(8,128)(2,1)S(1)}, u32[]{:S(2)}, u32[]{:S(2)}) collective-permute-start(bf16[2,2,64,384]{3,2,1,0:T(8,128)(2,1)S(1)} %copy-done.39), channel_id=1, source_target_pairs={{0,24},{8,16},{16,8},{24,0},{1,25},{9,17},{17,9},{25,1},{2,26},{10... | collective-permute-start | bytes 589832 | tf_op jit(solution)/shard_map/ppermute | solution.py:375
  124.2 55.6 %collective-permute-start.24 = (f32[2,2,6,384]{3,2,1,0:T(8,128)S(1)}, f32[2,2,6,384]{3,2,1,0:T(8,128)S(1)}, u32[]{:S(2)}, u32[]{:S(2)}) collective-permute-start(f32[2,2,6,384]{3,2,1,0:T(8,128)S(1)} %get-tuple-element.186), channel_id=1, source_target_pairs={{0,8},{8,0},{16,24},{24,16},{1,9},{9,1},{17,25},{25,17},{2,10},{10... | collective-permute-start | bytes 110600 | tf_op jit(solution)/shard_map/ppermute | solution.py:375
  124.3 55.7 %collective-permute-start.25 = (f32[2,2,6,384]{3,2,1,0:T(8,128)S(1)}, f32[2,2,6,384]{3,2,1,0:T(8,128)S(1)}, u32[]{:S(2)}, u32[]{:S(2)}) collective-permute-start(f32[2,2,6,384]{3,2,1,0:T(8,128)S(1)} %get-tuple-element.187), channel_id=1, source_target_pairs={{0,16},{8,24},{16,0},{24,8},{1,17},{9,25},{17,1},{25,9},{2,18},{10... | collective-permute-start | bytes 110600 | tf_op jit(solution)/shard_map/ppermute | solution.py:375
  125.0 56.4 %collective-permute-start.26 = (f32[2,2,6,384]{3,2,1,0:T(8,128)S(1)}, f32[2,2,6,384]{3,2,1,0:T(8,128)S(1)}, u32[]{:S(2)}, u32[]{:S(2)}) collective-permute-start(f32[2,2,6,384]{3,2,1,0:T(8,128)S(1)} %get-tuple-element.188), channel_id=1, source_target_pairs={{0,24},{8,16},{16,8},{24,0},{1,25},{9,17},{17,9},{25,1},{2,26},{10... | collective-permute-start | bytes 110600 | tf_op jit(solution)/shard_map/ppermute | solution.py:375
  126.2 60.0 %collective-permute-start.9 = (bf16[2,2,64,384]{3,2,1,0:T(8,128)(2,1)}, bf16[2,2,64,384]{3,2,1,0:T(8,128)(2,1)S(1)}, u32[]{:S(2)}, u32[]{:S(2)}) collective-permute-start(bf16[2,2,64,384]{3,2,1,0:T(8,128)(2,1)} %get-tuple-element.73), channel_id=1, source_target_pairs={{0,8},{8,0},{16,24},{24,16},{1,9},{9,1},{17,25},{25,17},{2,10},{10... | collective-permute-start | bytes 589832 | tf_op jit(solution)/shard_map/ppermute | solution.py:375
  126.5 60.8 %collective-permute-start.10 = (bf16[2,2,64,384]{3,2,1,0:T(8,128)(2,1)}, bf16[2,2,64,384]{3,2,1,0:T(8,128)(2,1)S(1)}, u32[]{:S(2)}, u32[]{:S(2)}) collective-permute-start(bf16[2,2,64,384]{3,2,1,0:T(8,128)(2,1)} %get-tuple-element.74), channel_id=1, source_target_pairs={{0,16},{8,24},{16,0},{24,8},{1,17},{9,25},{17,1},{25,9},{2,18},{10... | collective-permute-start | bytes 589832 | tf_op jit(solution)/shard_map/ppermute | solution.py:375
  189.5 30.8 %collective-permute-start.19 = (bf16[2,2,64,384]{3,2,1,0:T(8,128)(2,1)S(1)}, bf16[2,2,64,384]{3,2,1,0:T(8,128)(2,1)S(1)}, u32[]{:S(2)}, u32[]{:S(2)}) collective-permute-start(bf16[2,2,64,384]{3,2,1,0:T(8,128)(2,1)S(1)} %copy-done.42), channel_id=1, source_target_pairs={{0,16},{8,24},{16,0},{24,8},{1,17},{9,25},{17,1},{25,9},{2,18},{10... | collective-permute-start | bytes 589832 | tf_op jit(solution)/shard_map/ppermute | solution.py:375
  190.4 30.5 %collective-permute-start.20 = (bf16[2,2,64,384]{3,2,1,0:T(8,128)(2,1)}, bf16[2,2,64,384]{3,2,1,0:T(8,128)(2,1)S(1)}, u32[]{:S(2)}, u32[]{:S(2)}) collective-permute-start(bf16[2,2,64,384]{3,2,1,0:T(8,128)(2,1)} %get-tuple-element.98), channel_id=1, source_target_pairs={{0,24},{8,16},{16,8},{24,0},{1,25},{9,17},{17,9},{25,1},{2,26},{10... | collective-permute-start | bytes 589832 | tf_op jit(solution)/shard_map/ppermute | solution.py:375
  194.2 42.5 %collective-permute-start.21 = (bf16[2,2,64,384]{3,2,1,0:T(8,128)(2,1)}, bf16[2,2,64,384]{3,2,1,0:T(8,128)(2,1)S(1)}, u32[]{:S(2)}, u32[]{:S(2)}) collective-permute-start(bf16[2,2,64,384]{3,2,1,0:T(8,128)(2,1)} %get-tuple-element.102), channel_id=1, source_target_pairs={{0,8},{8,0},{16,24},{24,16},{1,9},{9,1},{17,25},{25,17},{2,10},{10... | collective-permute-start | bytes 589832 | tf_op jit(solution)/shard_map/ppermute | solution.py:375
  197.9 38.8 %collective-permute-start.22 = (bf16[2,2,64,384]{3,2,1,0:T(8,128)(2,1)}, bf16[2,2,64,384]{3,2,1,0:T(8,128)(2,1)S(1)}, u32[]{:S(2)}, u32[]{:S(2)}) collective-permute-start(bf16[2,2,64,384]{3,2,1,0:T(8,128)(2,1)} %get-tuple-element.103), channel_id=1, source_target_pairs={{0,16},{8,24},{16,0},{24,8},{1,17},{9,25},{17,1},{25,9},{2,18},{10... | collective-permute-start | bytes 589832 | tf_op jit(solution)/shard_map/ppermute | solution.py:375
  198.9 37.9 %collective-permute-start.23 = (bf16[2,2,64,384]{3,2,1,0:T(8,128)(2,1)}, bf16[2,2,64,384]{3,2,1,0:T(8,128)(2,1)S(1)}, u32[]{:S(2)}, u32[]{:S(2)}) collective-permute-start(bf16[2,2,64,384]{3,2,1,0:T(8,128)(2,1)} %get-tuple-element.104), channel_id=1, source_target_pairs={{0,24},{8,16},{16,8},{24,0},{1,25},{9,17},{17,9},{25,1},{2,26},{10... | collective-permute-start | bytes 589832 | tf_op jit(solution)/shard_map/ppermute | solution.py:375
  220.4 45.6 %collective-permute-start.48 = (bf16[576,1536]{1,0:T(8,128)(2,1)S(1)}, bf16[576,1536]{1,0:T(8,128)(2,1)S(1)}, u32[]{:S(2)}, u32[]{:S(2)}) collective-permute-start(bf16[576,1536]{1,0:T(8,128)(2,1)S(1)} %dynamic-slice_convert_fusion), channel_id=1, source_target_pairs={{0,8},{8,0},{16,24},{24,16},{1,9},{9,1},{17,25},{25,17},{2,10},{10... | collective-permute-start | bytes 5308424 | tf_op jit(solution)/shard_map/ppermute | solution.py:375
  266.7 25.1 %collective-permute-start.49 = (bf16[288,1536]{1,0:T(8,128)(2,1)S(1)}, bf16[288,1536]{1,0:T(8,128)(2,1)S(1)}, u32[]{:S(2)}, u32[]{:S(2)}) collective-permute-start(bf16[288,1536]{1,0:T(8,128)(2,1)S(1)} %dynamic-slice_convert_fusion.1), channel_id=1, source_target_pairs={{0,1},{1,0},{2,3},{3,2},{4,5},{5,4},{6,7},{7,6},{8,9},{9,8},{10,11... | collective-permute-start | bytes 2654216 | tf_op jit(solution)/shard_map/ppermute | solution.py:375
  350.1 38.8 %collective-permute-start.39 = (bf16[128,3456]{1,0:T(8,128)(2,1)S(1)}, bf16[128,3456]{1,0:T(8,128)(2,1)S(1)}, u32[]{:S(2)}, u32[]{:S(2)}) collective-permute-start(bf16[128,3456]{1,0:T(8,128)(2,1)S(1)} %pad_maximum_fusion.3), channel_id=1, source_target_pairs={{0,4},{1,5},{2,6},{3,7},{4,0},{5,1},{6,2},{7,3},{8,12},{9,13},{10,... | collective-permute-start | bytes 2654216 | tf_op jit(solution)/shard_map/ppermute | solution.py:375
  351.8 40.8 %collective-permute-start.47 = (bf16[192,1536]{1,0:T(8,128)(2,1)S(1)}, bf16[192,1536]{1,0:T(8,128)(2,1)S(1)}, u32[]{:S(2)}, u32[]{:S(2)}) collective-permute-start(bf16[192,1536]{1,0:T(8,128)(2,1)S(1)} %pad_maximum_fusion.5), channel_id=1, source_target_pairs={{0,8},{8,0},{16,24},{24,16},{1,9},{9,1},{17,25},{25,17},{2,10},{10... | collective-permute-start | bytes 1769480 | tf_op jit(solution)/shard_map/ppermute | solution.py:375
  369.2 26.1 %collective-permute-start.55 = (bf16[576,1536]{1,0:T(8,128)(2,1)S(1)}, bf16[576,1536]{1,0:T(8,128)(2,1)S(1)}, u32[]{:S(2)}, u32[]{:S(2)}) collective-permute-start(bf16[576,1536]{1,0:T(8,128)(2,1)S(1)} %pad_maximum_fusion.1), channel_id=1, source_target_pairs={{0,8},{8,0},{16,24},{24,16},{1,9},{9,1},{17,25},{25,17},{2,10},{10... | collective-permute-start | bytes 5308424 | tf_op jit(solution)/shard_map/ppermute | solution.py:375
  (81 other events, 683.5 us)

commit v2 on v1

v2 whole, which is shorter than its diff:
```python
import functools

import jax
import jax.numpy as jnp
from jax import lax
from jax.experimental import pallas as pl
from jax.experimental.pallas import tpu as pltpu
from jax.sharding import PartitionSpec as P

D = 384
HEADS = 6
HD = 64
MLP = 1536
F32 = jnp.float32
BF16 = jnp.bfloat16
CHUNKS = 2
GROUP = 16
VMEM = 58 * 2**20


def nn(a, b):
    return lax.dot_general(a, b, (((1,), (0,)), ((), ())), preferred_element_type=F32)


def nt(a, b):
    return lax.dot_general(a, b, (((1,), (1,)), ((), ())), preferred_element_type=F32)


def tn(a, b):
    return lax.dot_general(a, b, (((0,), (0,)), ((), ())), preferred_element_type=F32)


def cost(us):
    return pl.CostEstimate(flops=int(us * 1.0e9), bytes_accessed=1000, transcendentals=0)


def on_diagonal(pair):
    none = jnp.zeros_like(pair[:HD])
    return jnp.concatenate(
        [
            jnp.concatenate([pair[:HD], none], axis=1),
            jnp.concatenate([none, pair[HD:]], axis=1),
        ],
        axis=0,
    )


def norm_stats(x):
    c = x - jnp.mean(x, -1, keepdims=True)
    r = lax.rsqrt(jnp.mean(c * c, -1, keepdims=True) + 1e-6)
    return c * r, r


def norm_back(h, n, r):
    return r * (h - jnp.mean(h, -1, keepdims=True) - n * jnp.mean(h * n, -1, keepdims=True))


def divide(mine, acc, sent, kept):
    half = sent.shape[0]
    for j in range(half):
        sent[j] = acc[(1 - mine) * half + j].astype(BF16)
        kept[j] = acc[mine * half + j].astype(BF16)


def silu_low(v):
    v = v.astype(F32)
    return (v / (1.0 + jnp.exp(-v))).astype(BF16)


def spatial_fwd(start, idx, tok, cond, ada, w_t, wo, qkv_o, mix_o, br_o, tot_o, mod_o, *rest):
    slots, (scr, mod_s) = rest[:-2], rest[-2:]
    rows = slots[0].shape[2]
    frames = pl.num_programs(1)
    at = pl.program_id(0) * frames + pl.program_id(1)

    @pl.when(at == 0)
    def _():
        mod_s[...] = nn(silu_low(cond[...]), ada[...])

    at = at + start * frames
    md = [mod_s[pl.ds(at, 1), j * D : (j + 1) * D] for j in range(3)]
    for j in range(3):
        mod_o[0, 0, j : j + 1] = md[j]
    x = tok[0, 0].astype(F32)
    n, _ = norm_stats(x)
    first = (n * (1.0 + md[1]) + md[0]).astype(BF16)
    qkv_o[0, 0] = nt(w_t[...], first).astype(BF16)
    for j in range(HEADS // 2):
        a = j * 2 * HD
        q = on_diagonal(qkv_o[0, 0, a : a + 2 * HD] * BF16(0.125))
        k = qkv_o[0, 0, D + a : D + a + 2 * HD]
        s = tn(k, q)
        mx = jnp.max(s, axis=0, keepdims=True)
        p = jnp.exp(s - mx)
        total = jnp.sum(p, axis=0, keepdims=True)
        tot_o[0, 0, j : j + 1] = mx + jnp.log(total)
        p = p.astype(BF16)
        scale = 1.0 / total
        cut = q.shape[1] // 2
        for e in range(2):
            v = qkv_o[0, 0, 2 * D + a + e * HD : 2 * D + a + (e + 1) * HD]
            cols = slice(e * cut, (e + 1) * cut)
            mix_o[0, 0, a + e * HD : a + (e + 1) * HD] = (nn(v, p[:, cols]) * scale[:, cols]).astype(BF16)
    br = tn(mix_o[0, 0], wo[...])
    br_o[0, 0] = br.astype(BF16)
    scr[...] = (x + md[2] * br).astype(BF16)
    i = idx[0]
    for k, slot in enumerate(slots):
        slot[0, 0] = scr[pl.ds(pl.multiple_of((i ^ k) * rows, GROUP), rows), :]


def call_spatial_fwd(idx, tok, cond, ada, w_t, wo, start, count, n):
    f = tok.shape[1]
    p = tok.shape[2]
    whole = lambda *s: pl.BlockSpec((1, 1) + s, lambda b, f, i: (b + start, f) + (0,) * len(s))
    part = lambda *s: pl.BlockSpec((1, 1) + s, lambda b, f, i: (b, f) + (0,) * len(s))
    fixed = lambda *s: pl.BlockSpec(s, lambda b, f, i: (0,) * len(s), pipeline_mode=pl.Buffered(1))
    sd = lambda s, d: jax.ShapeDtypeStruct((count, f) + s, d)
    return pl.pallas_call(
        functools.partial(spatial_fwd, start),
        grid_spec=pltpu.PrefetchScalarGridSpec(
            num_scalar_prefetch=1,
            grid=(count, f),
            in_specs=[whole(p, D), fixed(tok.shape[0] * f, D), fixed(D, 3 * D), fixed(3 * D, D), fixed(D, D)],
            out_specs=[part(3 * D, p), part(D, p), part(p, D), part(HEADS // 2, 2 * p), part(3, D)]
            + [part(p // n, D)] * n,
            scratch_shapes=[pltpu.VMEM((p, D), BF16), pltpu.VMEM((tok.shape[0] * f, 3 * D), F32)],
        ),
        out_shape=[sd((3 * D, p), BF16), sd((D, p), BF16), sd((p, D), BF16)]
        + [sd((HEADS // 2, 2 * p), F32), sd((3, D), F32)]
        + [sd((p // n, D), BF16)] * n,
        compiler_params=pltpu.CompilerParams(vmem_limit_bytes=VMEM),
        cost_estimate=cost(6 * count),
        name="spatial_fwd",
    )(idx, tok, cond.reshape(-1, D), ada, w_t, wo)


def gather_tile(refs, groups):
    f = refs[0].shape[1]
    return jnp.concatenate(
        [
            r[0, j, g * GROUP : (g + 1) * GROUP, :]
            for g in range(groups)
            for r in refs
            for j in range(f)
        ],
        axis=0,
    )


def scatter_tile(refs, value, groups, f):
    at = 0
    for g in range(groups):
        for r in refs:
            for j in range(f):
                r[0, j, g * GROUP : (g + 1) * GROUP, :] = value[at : at + GROUP]
                at += GROUP


def middle(n, start, first_chunk, last_chunk, idx, seg, *refs):
    refs = list(refs)
    a1, refs = refs[:n], refs[n:]
    ct, refs = refs[:n], refs[n:]
    cond, ada_a, ada_b, tq_t, tq, to, up, down = refs[:8]
    refs = refs[8:]
    if not first_chunk:
        init, refs = refs[0], refs[3:]
    dl, refs = refs[:n], refs[n:]
    ou = [refs[k // (n // 2)].at[k % (n // 2)] for k in range(n)]
    refs = refs[2:]
    gsum = refs[0]
    if last_chunk:
        sent, kept = refs[1:3]
        refs = refs[3:]
        acc = refs.pop()
    else:
        acc = refs[1]
        refs = refs[2:]
    mod_s, qkv_s, p_s, mix_s, dg_s, hid_s, dqkv_s = refs
    groups = a1[0].shape[2] // GROUP
    frames = n * a1[0].shape[1]
    span = frames * GROUP
    tokens = span * groups

    @pl.when(pl.program_id(0) == 0)
    def _():
        acc[...] = jnp.zeros_like(acc) if first_chunk else init[...]

    act = silu_low(cond[0])
    mod_s[:, : 3 * D] = nn(act, ada_a[...])
    mod_s[:, 3 * D :] = nn(act, ada_b[...])

    def per_frame(piece, plus=0.0):
        rows = [mod_s[t : t + 1, piece * D : (piece + 1) * D] + plus for t in range(frames)]
        one = jnp.concatenate([jnp.broadcast_to(r, (GROUP, D)) for r in rows], axis=0)
        return jnp.concatenate([one] * groups, axis=0)

    def frame_sum(v):
        return jnp.sum(jnp.sum(v.reshape(groups, frames, GROUP, D), axis=0), axis=1)

    def add(base, col, value):
        for j in range(value.shape[1] // D):
            acc[base + col // D + j] += value[:, j * D : (j + 1) * D]

    x1 = gather_tile(a1, groups).astype(F32)
    n2, r2 = norm_stats(x1)
    second = (n2 * per_frame(1, 1.0) + per_frame(0)).astype(BF16)
    qkv_s[...] = nt(tq_t[...], second).astype(BF16)
    lane = lax.broadcasted_iota(jnp.int32, (span, span), 0) % GROUP
    other = lax.broadcasted_iota(jnp.int32, (span, span), 1) % GROUP
    segs = [seg[pl.program_id(0) + start, t] for t in range(frames)]

    def segment_of(axis):
        at = lax.broadcasted_iota(jnp.int32, (span, span), axis) // GROUP
        value = jnp.zeros((span, span), jnp.int32)
        for t in range(frames):
            value = jnp.where(at == t, segs[t], value)
        return value

    allowed = (segment_of(0) == segment_of(1)) & (lane == other)
    bias = jnp.where(allowed, 0.0, -1e30)
    bias2 = jnp.concatenate([bias, bias], axis=1)
    for g in range(groups):
        cols = slice(g * span, (g + 1) * span)
        for j in range(HEADS // 2):
            a = j * 2 * HD
            q = on_diagonal(qkv_s[a : a + 2 * HD, cols] * BF16(0.125))
            k = qkv_s[D + a : D + a + 2 * HD, cols]
            v = qkv_s[2 * D + a : 2 * D + a + 2 * HD, cols]
            s = tn(k, q) + bias2
            p = jnp.exp(s - jnp.max(s, axis=0, keepdims=True))
            p = p * (1.0 / jnp.sum(p, axis=0, keepdims=True))
            p_s[g * (HEADS // 2) + j] = p
            o = nn(v, p.astype(BF16)).astype(BF16)
            mix_s[a : a + HD, cols] = o[:HD, :span]
            mix_s[a + HD : a + 2 * HD, cols] = o[HD:, span:]
    br2 = tn(mix_s[...], to[...])
    x2 = x1 + per_frame(2) * br2
    n3, r3 = norm_stats(x2)
    third = (n3 * per_frame(4, 1.0) + per_frame(3)).astype(BF16)
    step = 2 * D
    br3 = jnp.zeros((tokens, D), F32)
    for c in range(0, MLP, step):
        pre = nn(third, up[:, c : c + step])
        sq = pre * pre
        t = jnp.tanh(pre * (0.7978845608028654 + (0.7978845608028654 * 0.044715) * sq))
        half = 0.5 + 0.5 * t
        hid = (pre * half).astype(BF16)
        hid_s[:, c : c + step] = hid
        inner = 0.7978845608028654 + (3 * 0.7978845608028654 * 0.044715) * sq
        dg_s[:, c : c + step] = half + 0.5 * pre * (1.0 - t * t) * inner
        br3 += nn(hid, down[c : c + step, :])
    gate3 = per_frame(5)
    scatter_tile(ou, (x2 + gate3 * br3).astype(BF16), groups, a1[0].shape[1])
    cot = gather_tile(ct, groups).astype(F32)
    gsum[0, :, 5] = frame_sum(cot * br3)
    gb3 = (gate3 * cot).astype(BF16)
    gb3_t = gb3.T
    third_t = third.T
    g3 = jnp.zeros((tokens, D), F32)
    for c in range(0, MLP, step):
        add(4, c, nn(gb3_t, hid_s[:, c : c + step]))
        gp = (nt(gb3, down[c : c + step, :]) * dg_s[:, c : c + step]).astype(BF16)
        add(0, c, nn(third_t, gp))
        g3 += nt(gp, up[:, c : c + step])
    gsum[0, :, 3] = frame_sum(g3)
    gsum[0, :, 4] = frame_sum(g3 * n3)
    dx3 = norm_back(g3 * per_frame(4, 1.0), n3, r3)
    ga2 = cot + dx3
    gsum[0, :, 2] = frame_sum(ga2 * br2)
    gb2 = (per_frame(2) * ga2).astype(BF16)
    add(11, 0, nn(mix_s[...], gb2))
    gm_t = nt(to[...], gb2).astype(BF16)
    for g in range(groups):
        cols = slice(g * span, (g + 1) * span)
        for j in range(HEADS // 2):
            a = j * 2 * HD
            q = on_diagonal(qkv_s[a : a + 2 * HD, cols] * BF16(0.125))
            k = qkv_s[D + a : D + a + 2 * HD, cols]
            v = qkv_s[2 * D + a : 2 * D + a + 2 * HD, cols]
            go = on_diagonal(gm_t[a : a + 2 * HD, cols])
            p = p_s[g * (HEADS // 2) + j]
            dp = tn(v, go)
            ds = (p * (dp - jnp.sum(p * dp, axis=0, keepdims=True))).astype(BF16)
            dqkv_s[2 * D + a : 2 * D + a + 2 * HD, cols] = nt(go, p.astype(BF16)).astype(BF16)
            dqkv_s[D + a : D + a + 2 * HD, cols] = nt(q, ds).astype(BF16)
            dq = (nn(k, ds) * 0.125).astype(BF16)
            dqkv_s[a : a + HD, cols] = dq[:HD, :span]
            dqkv_s[a + HD : a + 2 * HD, cols] = dq[HD:, span:]
    dqkv = dqkv_s[...]
    add(8, 0, nt(second.T, dqkv))
    g2 = nn(tq[...], dqkv).T
    gsum[0, :, 0] = frame_sum(g2)
    gsum[0, :, 1] = frame_sum(g2 * n2)
    dx2 = norm_back(g2 * per_frame(1, 1.0), n2, r2)
    scatter_tile(dl, (dx3 + dx2).astype(BF16), groups, a1[0].shape[1])
    if last_chunk:

        @pl.when(pl.program_id(0) == pl.num_programs(0) - 1)
        def _():
            divide(idx[0] & 1, acc, sent, kept)


def sum_specs(last_chunk, blocks):
    const = lambda *s: pl.BlockSpec(s, lambda *g: (0,) * len(s))
    sd = jax.ShapeDtypeStruct
    if not last_chunk:
        return [const(blocks, D, D)], [sd((blocks, D, D), F32)], []
    half = (blocks // 2, D, D)
    return [const(*half)] * 2, [sd(half, BF16), sd(half, BF16)], [pltpu.VMEM((blocks, D, D), F32)]


def call_middle(idx, seg, a1, ct, cond, ada, tq_t, tq, to, up, down, init, start, last_chunk):
    n = len(a1)
    count, f, rows = a1[0].shape[:3]
    packs = cond.shape[0]
    frames = n * f
    span = frames * GROUP
    tokens = frames * rows
    groups = rows // GROUP
    part = lambda *s: pl.BlockSpec((1,) + s, lambda b, i, s_: (b,) + (0,) * len(s))
    whole = lambda *s: pl.BlockSpec((1,) + s, lambda b, i, s_: (b + start,) + (0,) * len(s))
    fixed = lambda *s: pl.BlockSpec(s, lambda b, i, s_: (0,) * len(s), pipeline_mode=pl.Buffered(1))
    column = lambda j: pl.BlockSpec((D, 3 * D), lambda b, i, s_: (0, j), pipeline_mode=pl.Buffered(1))
    sd = jax.ShapeDtypeStruct
    sum_out, sum_shape, sum_scratch = sum_specs(last_chunk, 12)
    stack = (n // 2, packs, f, rows, D)
    stacked = pl.BlockSpec((n // 2, 1, f, rows, D), lambda b, i, s_: (0, b + start, 0, 0, 0))
    return pl.pallas_call(
        functools.partial(middle, n, start, not init, last_chunk),
        grid_spec=pltpu.PrefetchScalarGridSpec(
            num_scalar_prefetch=2,
            grid=(count,),
            in_specs=[part(f, rows, D)] * n
            + [whole(f, rows, D)] * n
            + [whole(frames, D)]
            + [column(1), column(2), fixed(3 * D, D), fixed(D, 3 * D)]
            + [fixed(D, D), fixed(D, MLP), fixed(MLP, D)]
            + ([fixed(12, D, D)] + [pl.BlockSpec(memory_space=pl.ANY)] * 2 if init else []),
            out_specs=[part(f, rows, D)] * n + [stacked] * 2 + [part(frames, 6, D)] + sum_out,
            scratch_shapes=[
                pltpu.VMEM((frames, 6 * D), F32),
                pltpu.VMEM((3 * D, tokens), BF16),
                pltpu.VMEM((groups * HEADS // 2, span, 2 * span), F32),
                pltpu.VMEM((D, tokens), BF16),
                pltpu.VMEM((tokens, MLP), F32),
                pltpu.VMEM((tokens, MLP), BF16),
                pltpu.VMEM((3 * D, tokens), BF16),
            ]
            + sum_scratch,
        ),
        out_shape=[sd((count, f, rows, D), BF16)] * n
        + [sd(stack, BF16)] * 2
        + [sd((count, frames, 6, D), F32)]
        + sum_shape,
        input_output_aliases={2 + 2 * n + 9 + j: n + j for j in range(2)} if init else {},
        compiler_params=pltpu.CompilerParams(vmem_limit_bytes=VMEM),
        cost_estimate=cost(16 * count),
        name="middle",
    )(idx, seg, *a1, *ct, cond, ada, ada, tq_t, tq, to, up, down, *init)


def spatial_bwd(n, first_chunk, last_chunk, idx, tok, cot, mod, qkv, mix, br, tot, wo, *rest):
    rest = list(rest)
    if not first_chunk:
        init, rest = rest[0], rest[1:]
    dl, rest = rest[:n], rest[n:]
    dqkv_o, ga_o, gg_o = rest[:3]
    if last_chunk:
        sent, kept, scr, acc = rest[3:]
    else:
        acc, scr = rest[3:]

    @pl.when((pl.program_id(0) == 0) & (pl.program_id(1) == 0))
    def _():
        acc[...] = jnp.zeros_like(acc) if first_chunk else init[...]

    rows = dl[0].shape[2]
    i = idx[0]
    for k in range(n):
        scr[pl.ds(pl.multiple_of((i ^ k) * rows, GROUP), rows), :] = dl[k][0, 0]
    ga = cot[0, 0].astype(F32) + scr[...].astype(F32)
    ga_o[0, 0] = ga
    md = mod[0, 0]
    gg_o[0, 0] = jnp.sum(ga * br[0, 0].astype(F32), axis=0, keepdims=True)
    gb = (md[2:3] * ga).astype(BF16)
    acc[3] += nn(mix[0, 0], gb)
    gm = nt(wo[...], gb).astype(BF16)
    for j in range(HEADS // 2):
        a = j * 2 * HD
        q = qkv[0, 0, a : a + 2 * HD] * BF16(0.125)
        k = qkv[0, 0, D + a : D + a + 2 * HD]
        v = qkv[0, 0, 2 * D + a : 2 * D + a + 2 * HD]
        go = gm[a : a + 2 * HD]
        p = jnp.exp(tn(k, on_diagonal(q)) - tot[0, 0, j : j + 1])
        dp = tn(v, on_diagonal(go))
        ds = (p * (dp - jnp.sum(p * dp, axis=0, keepdims=True))).astype(BF16)
        p = p.astype(BF16)
        cut = q.shape[1]
        for e in range(2):
            cols = slice(e * cut, (e + 1) * cut)
            r = slice(e * HD, (e + 1) * HD)
            at = a + e * HD
            dqkv_o[0, 0, 2 * D + at : 2 * D + at + HD] = nt(go[r], p[:, cols]).astype(BF16)
            dqkv_o[0, 0, D + at : D + at + HD] = nt(q[r], ds[:, cols]).astype(BF16)
            dqkv_o[0, 0, at : at + HD] = (nn(k[r], ds[:, cols]) * 0.125).astype(BF16)
    nrm, _ = norm_stats(tok[0, 0].astype(F32))
    first = (nrm * (1.0 + md[1:2]) + md[0:1]).astype(BF16)
    value = nt(first.T, dqkv_o[0, 0])
    for j in range(3):
        acc[j] += value[:, j * D : (j + 1) * D]
    if last_chunk:
        end = (pl.program_id(0) == pl.num_programs(0) - 1) & (pl.program_id(1) == pl.num_programs(1) - 1)

        @pl.when(end)
        def _():
            divide(i & 1, acc, sent, kept)


def call_spatial_bwd(idx, tok, cot, mod, qkv, mix, br, tot, wo, init, dl, start, last_chunk):
    n = len(dl)
    count, f, rows = dl[0].shape[:3]
    p = tok.shape[2]
    whole = lambda *s: pl.BlockSpec((1, 1) + s, lambda b, f, i: (b + start, f) + (0,) * len(s))
    part = lambda *s: pl.BlockSpec((1, 1) + s, lambda b, f, i: (b, f) + (0,) * len(s))
    fixed = lambda *s: pl.BlockSpec(s, lambda b, f, i: (0,) * len(s), pipeline_mode=pl.Buffered(1))
    sd = lambda s, d: jax.ShapeDtypeStruct((count, f) + s, d)
    sum_out, sum_shape, sum_scratch = sum_specs(last_chunk, 4)
    return pl.pallas_call(
        functools.partial(spatial_bwd, n, not init, last_chunk),
        grid_spec=pltpu.PrefetchScalarGridSpec(
            num_scalar_prefetch=1,
            grid=(count, f),
            in_specs=[whole(p, D), whole(p, D), part(3, D), part(3 * D, p), part(D, p)]
            + [part(p, D), part(HEADS // 2, 2 * p), fixed(D, D)]
            + [fixed(4, D, D)] * len(init)
            + [part(rows, D)] * n,
            out_specs=[part(3 * D, p), part(p, D), part(1, D)]
            + sum_out,
            scratch_shapes=[pltpu.VMEM((p, D), BF16)] + sum_scratch,
        ),
        out_shape=[sd((3 * D, p), BF16), sd((p, D), F32), sd((1, D), F32)]
        + sum_shape,
        compiler_params=pltpu.CompilerParams(vmem_limit_bytes=VMEM),
        cost_estimate=cost(6 * count),
        name="spatial_bwd",
    )(idx, tok, cot, mod, qkv, mix, br, tot, wo, *init, *dl)


def last_step(masks, idx, tok, mod, w_t, dqkv, ga, *rest):
    grad_o, out_o, gs_o = rest[-3:]
    rows = rest[0].shape[3]
    i = idx[0]
    for k, piece in zip(masks, rest):
        out_o[0, 0, pl.ds(pl.multiple_of((i ^ k) * rows, GROUP), rows), :] = piece[0, 0, 0]
    g = tn(dqkv[0, 0], w_t[...])
    nrm, r = norm_stats(tok[0, 0].astype(F32))
    md = mod[0, 0]
    gs_o[0, 0, 0:1] = jnp.sum(g, axis=0, keepdims=True)
    gs_o[0, 0, 1:2] = jnp.sum(g * nrm, axis=0, keepdims=True)
    grad_o[0, 0] = ga[0, 0] + norm_back(g * (1.0 + md[1:2]), nrm, r)


def call_last(idx, tok, mod, w_t, dqkv, ga, ou, start, held):
    n = len(ou)
    arrays, offsets, masks = zip(*ou)
    count, f = dqkv.shape[:2]
    rows = arrays[0].shape[3]
    p = tok.shape[2]
    whole = lambda *s: pl.BlockSpec((1, 1) + s, lambda b, f, i: (b + start, f) + (0,) * len(s))
    part = lambda *s: pl.BlockSpec((1, 1) + s, lambda b, f, i: (b, f) + (0,) * len(s))
    fixed = lambda *s: pl.BlockSpec(s, lambda b, f, i: (0,) * len(s), pipeline_mode=pl.Buffered(1))
    piece = lambda j: pl.BlockSpec((1, 1, 1, rows, D), lambda b, f, i: (j, b + start, f, 0, 0))
    sd = lambda s, d: jax.ShapeDtypeStruct((count, f) + s, d)
    return pl.pallas_call(
        functools.partial(last_step, masks),
        grid_spec=pltpu.PrefetchScalarGridSpec(
            num_scalar_prefetch=1,
            grid=(count, f),
            in_specs=[whole(p, D), part(3, D), fixed(3 * D, D), part(3 * D, p), part(p, D)]
            + [piece(j) for j in offsets]
            + [pl.BlockSpec(memory_space=pl.ANY)] * len(held),
            out_specs=[whole(p, D), whole(p, D), part(2, D)],
        ),
        out_shape=[
            jax.ShapeDtypeStruct(tok.shape, F32),
            jax.ShapeDtypeStruct(tok.shape, BF16),
            sd((2, D), F32),
        ],
        input_output_aliases={6 + n + j: j for j in range(len(held))},
        compiler_params=pltpu.CompilerParams(vmem_limit_bytes=VMEM),
        cost_estimate=cost(3 * count),
        name="last_step",
    )(idx, tok, mod, w_t, dqkv, ga, *arrays, *held)


def pick(idx, own, other):
    mine = idx[0] & 1
    half = own.shape[0]
    return lambda k: jnp.where(k // half == mine, own[k % half], other[k % half]).astype(F32)


def finish_early(idx, own, other, up_o, down_o, qkv_o, out_o):
    block = pick(idx, own, other)
    for j in range(4):
        up_o[:, j * D : (j + 1) * D] = block(j)
        down_o[j * D : (j + 1) * D, :] = block(4 + j).T
    for j in range(3):
        qkv_o[:, j * D : (j + 1) * D] = block(8 + j)
    out_o[...] = block(11)


def call_finish_early(idx, own, other):
    sd = lambda *s: jax.ShapeDtypeStruct(s, F32)
    return pl.pallas_call(
        finish_early,
        in_specs=[pl.BlockSpec(memory_space=pltpu.SMEM)] + [pl.BlockSpec(memory_space=pltpu.VMEM)] * 2,
        out_specs=[pl.BlockSpec(memory_space=pltpu.VMEM)] * 4,
        out_shape=[sd(D, MLP), sd(MLP, D), sd(D, 3 * D), sd(D, D)],
        compiler_params=pltpu.CompilerParams(vmem_limit_bytes=VMEM),
        cost_estimate=cost(3),
        name="finish_early",
    )(idx, own, other)


def finish_late(idx, own, other, rest, mod, ada_o, qkv_o, out_o):
    block = pick(idx, own, other)
    act = silu_low(rest[:, 6 * D :]).T
    ada_o[:, : 3 * D] = nn(act, mod[...])
    ada_o[:, 3 * D :] = nn(act, rest[:, : 6 * D])
    for j in range(3):
        qkv_o[:, j * D : (j + 1) * D] = block(j)
    out_o[...] = block(3)


def call_finish_late(idx, own, other, rest, mod):
    sd = lambda *s: jax.ShapeDtypeStruct(s, F32)
    return pl.pallas_call(
        finish_late,
        in_specs=[pl.BlockSpec(memory_space=pltpu.SMEM)] + [pl.BlockSpec(memory_space=pltpu.VMEM)] * 4,
        out_specs=[pl.BlockSpec(memory_space=pltpu.VMEM)] * 3,
        out_shape=[sd(D, 9 * D), sd(D, 3 * D), sd(D, D)],
        compiler_params=pltpu.CompilerParams(vmem_limit_bytes=VMEM),
        cost_estimate=cost(4),
        name="finish_late",
    )(idx, own, other, rest, mod)


def swap(x, axis, mask):
    size = lax.axis_size(axis)
    return lax.ppermute(x, axis, [(s, s ^ mask) for s in range(size)])


def bits_of(axis):
    return [(axis, b) for b in range(lax.axis_size(axis).bit_length() - 1)]


def bit_of(axis, b):
    return (lax.axis_index(axis) >> b) & 1


def orders():
    path = bits_of("pack") + bits_of("frame")[1:]
    path = path[:1] + path[-1:] + path[1:-1]
    half = len(path) // 2
    return path, path[half:] + path[:half]


def swap_by_core(x, step):
    nf, npk = lax.axis_size("frame"), lax.axis_size("pack")
    perm = []
    for pack in range(npk):
        for frame in range(nf):
            axis, b = step[frame & 1]
            to = (pack ^ (1 << b), frame) if axis == "pack" else (pack, frame ^ (1 << b))
            perm.append((frame * npk + pack, to[1] * npk + to[0]))
    return lax.ppermute(x, ("frame", "pack"), perm)


def ar_steps():
    core = ("frame", 0)
    return [(core, core)] + list(zip(*orders()))


def bit_by_core(step):
    core = bit_of("frame", 0)
    return jnp.where(core == 0, bit_of(*step[0]), bit_of(*step[1]))


def split(g, step):
    mine = bit_by_core(step)
    half = g.shape[0] // 2
    send = lax.dynamic_slice_in_dim(g, (1 - mine) * half, half, 0)
    return send, lax.dynamic_slice_in_dim(g, mine * half, half, 0)


def double(g, step):
    other = swap_by_core(g, step)
    mine = bit_by_core(step) == 1
    return jnp.concatenate([jnp.where(mine, other, g), jnp.where(mine, g, other)], axis=0)


class Regroup:
    def __init__(self, lo, hi):
        self.count = lo.shape[0]
        self.pieces = [(lo, 0, 0)]
        self.start(hi)

    def start(self, send):
        self.moving = swap(send, "frame", self.count)

    def arrive(self, after=None):
        got = self.moving if after is None else tie(self.moving, after)
        k = self.count
        self.pieces += [(got, j * k, m ^ k) for j, (_, _, m) in enumerate(self.pieces)]
        if k > 1:
            half = k // 2
            send = jnp.concatenate([a[o + half : o + k] for a, o, _ in self.pieces], axis=0)
            self.count = half
            self.start(send)
            return False
        return True


def reduce_slots(v):
    while v.shape[1] > 1:
        half = v.shape[1] // 2
        v = v[:, :half] + swap(v[:, half:], "frame", half)
    return v[:, 0]


class Summing:
    def __init__(self, send, keep):
        self.todo = ar_steps()
        self.done = []
        self.send, self.keep = send, keep
        self.moving = None
        self.value = None

    def start(self):
        step = self.todo[0]
        if self.value is not None:
            self.send, self.keep = split(self.value, step)
        self.moving = swap_by_core(self.send, step)
        return self

    def add(self, after=None):
        moving = self.moving if after is None else tie(self.moving, after)
        self.value = (self.keep.astype(F32) + moving.astype(F32)).astype(BF16)
        self.done.append(self.todo.pop(0))
        return self.value

    def finish_halving(self):
        while self.todo:
            self.start()
            self.add()

    def finish_doubling(self):
        g = self.value
        for step in self.done[:0:-1]:
            g = double(g, step)
        return g, swap_by_core(g, self.done[0])


def spread(g, steps, after=None):
    for axis, b in steps:
        other = swap(g, axis, 1 << b)
        if after is not None:
            other = tie(other, after)
        mine = bit_of(axis, b) == 1
        g = jnp.concatenate([jnp.where(mine, other, g), jnp.where(mine, g, other)], axis=0)
    return g


def tie_all(values, *deps):
    return list(lax.optimization_barrier((*values, *deps))[: len(values)])


def tie(value, *deps):
    return lax.optimization_barrier((value, *deps))[0]


def local(
    tokens,
    condition,
    clip_lengths,
    ada_weight,
    spatial_qkv,
    spatial_out,
    temporal_qkv,
    temporal_out,
    mlp_up,
    mlp_down,
    cotangent,
):
    n = lax.axis_size("frame")
    i = lax.axis_index("frame")
    idx = i.reshape(1).astype(jnp.int32)
    packs, f, patches = tokens.shape[:3]
    rows = patches // n
    count = packs // CHUNKS
    every = bits_of("frame") + bits_of("pack")

    cut = lambda v, k: lax.dynamic_slice_in_dim(v, (i ^ k) * rows, rows, 2)
    send = lambda parts: [parts[0]] + [swap(parts[k], "frame", k) for k in range(1, n)]
    steps = ar_steps()

    sq_t = spatial_qkv.T
    tq_t = temporal_qkv.T
    ct = send([cut(cotangent, k) for k in range(n)])
    top = n // 2
    cond_slots, masks = condition[None], [0]
    cond_slots = jnp.concatenate([cond_slots, swap(cond_slots, "frame", top)], axis=0)
    masks = masks + [m ^ top for m in masks]
    frame_ids = jnp.concatenate([(i ^ k) * f + jnp.arange(f, dtype=jnp.int32) for k in range(n)])
    width = clip_lengths.shape[1]
    ends = [jnp.sum(clip_lengths[:, : j + 1], axis=1) for j in range(width)]
    segment = sum((e[:, None] <= frame_ids[None, :]).astype(jnp.int32) for e in ends)

    fwd = []
    source = tokens
    for c in range(CHUNKS):
        res = call_spatial_fwd(idx, source, condition, ada_weight, sq_t, spatial_out, c * count, count, n)
        slots = list(res[5:])
        if c:
            cond_slots = tie(cond_slots, res[4], fwd[-1][1][1])
            while top > 1:
                top //= 2
                cond_slots = jnp.concatenate([cond_slots, swap(cond_slots, "frame", top)], axis=0)
                masks = masks + [m ^ top for m in masks]
            cond_slots = jnp.stack([cond_slots[masks.index(k)] for k in range(n)], axis=1)
            cond_slots = cond_slots.reshape(packs, n * f, D)
            slots = tie_all(slots, *fwd[-1][1][1:], *ct[1:], cond_slots)
        fwd.append((res[:5], send(slots)))
        if c == 0:
            source = tie(tokens, cond_slots, segment, tq_t, ct[1])

    init, mids = [], []
    for c in range(CHUNKS):
        last = c == CHUNKS - 1
        res = call_middle(
            idx, segment, fwd[c][1], ct, cond_slots, ada_weight, tq_t, temporal_qkv, temporal_out,
            mlp_up, mlp_down, init, c * count, last,
        )
        init = [res[n + 3], res[n], res[n + 1]]
        res = list(res)
        if c:
            res = tie_all(res, *mids[-1][0][1:])
        mids.append((send(res[:n]), res[n + 2]))
    flat = lambda v: v.reshape(-1, D)
    early = Summing(flat(res[n + 3]), flat(res[n + 4])).start()
    outs = Regroup(res[n], res[n + 1])

    acc, backs = [], []
    for c in range(CHUNKS):
        last = c == CHUNKS - 1
        qkv, mix, br, tot, mod = fwd[c][0]
        dl = mids[c][0]
        if c:
            early.add(after=backs[-1][2])
            early.start()
            dl = [tie(v, early.send) for v in dl]
        res = call_spatial_bwd(
            idx, tokens, cotangent, mod, qkv, mix, br, tot, spatial_out, acc, dl, c * count, last
        )
        acc = list(res[3:])
        backs.append(res)
    sums = jnp.concatenate([m[1] for m in mids], 0).reshape(packs, n, f, 6, D)
    sums = reduce_slots(tie(sums, backs[0][2]))
    late = Summing(flat(acc[0]), flat(acc[1])).start()
    early.add(after=backs[-1][2])
    early.start()
    every = bits_of("pack") + bits_of("frame")[::-1]
    low = tie(sums, backs[-1][2]).astype(BF16).reshape(packs * f, 6 * D)
    while not outs.arrive(after=backs[-1][2]):
        pass
    rest_all = jnp.concatenate([low, condition.reshape(packs * f, D)], axis=1)
    lasts, held = [], []
    for c in range(CHUNKS):
        dqkv, ga, gate_sum = backs[c][:3]
        ga = tie(ga, early.send) if c == 0 else tie(ga, early.send, late.send)
        res = call_last(idx, tokens, fwd[c][0][4], sq_t, dqkv, ga, outs.pieces, c * count, held)
        held = list(res[:2])
        lasts.append(res)
        rest_all = spread(rest_all, every[c : c + 1], after=res[2])
        late.add(after=res[2])
        late.start()
        early.add(after=res[2])
        if early.todo:
            early.start()
    if early.todo and early.moving is not None:
        early.add()
    late.add()
    early.finish_halving()
    late.finish_halving()
    grad_tokens, output = held

    rest_all = spread(rest_all, every[CHUNKS:])
    own = jnp.concatenate(
        [jnp.concatenate([lasts[c][2], backs[c][2]], axis=2) for c in range(CHUNKS)], axis=0
    ).astype(BF16)
    own = own.reshape(packs * f, 3 * D)
    mod_all = spread(own, every)
    dot = functools.partial(jnp.einsum, preferred_element_type=F32)
    grad_mod = jnp.concatenate([own, low], axis=1)
    back = dot("tj,ij->ti", grad_mod, ada_weight).reshape(packs, f, D)
    cf = condition.astype(F32)
    sig = 1.0 / (1.0 + jnp.exp(-cf))
    grad_condition = back * (sig * (1.0 + cf * (1.0 - sig)))

    blocks = lambda v: v.reshape(-1, D, D)
    e_own, e_other = early.finish_doubling()
    l_own, l_other = late.finish_doubling()
    up, down, t_qkv, t_out = call_finish_early(idx, blocks(e_own), blocks(e_other))
    ada, s_qkv, s_out = call_finish_late(idx, blocks(l_own), blocks(l_other), rest_all, mod_all)
    return (output, grad_tokens, grad_condition, ada, s_qkv, s_out, t_qkv, t_out, up, down)


def solution(mesh):
    tok = P("pack", "frame", None, None)
    cond = P("pack", "frame", None)
    return jax.shard_map(
        local,
        mesh=mesh,
        in_specs=(tok, cond, P("pack", None), P(), P(), P(), P(), P(), P(), P(), tok),
        out_specs=(tok, tok, cond, P(), P(), P(), P(), P(), P(), P()),
        check_vma=False,
    )
```

time: 410 us -> 280 us (0.68)
  waiting for transfers between devices: 143 us -> 50.9 us
  Pallas kernels: 163 us -> 142 us
  local copies, waits for them, and re-layouts: 25.4 us -> 14.5 us
  matrix products: 9.81 us -> 0.79 us
    ppermute x56 -> x31, waiting for transfers between devices: 143 us -> 15.9 us  [swap(): return lax.ppermute(x, axis, [(s, s ^ mask) for s in range(size)])]
    ppermute x0 -> x20, waiting for transfers between devices: none -> 35 us  [swap_by_core(): return lax.ppermute(x, ('frame', 'pack'), perm)]
    pallas_call x8 -> x10, Pallas kernels: 163 us -> 142 us  [the longest x2 67.8 us: call_middle(): pl.pallas_call(functools.partial(middle, n, start, not init, last_chunk),...]
    ppermute x0 -> x20, starting transfers between devices: none -> 16.8 us  [swap_by_core(): return lax.ppermute(x, ('frame', 'pack'), perm)]
    ppermute x56 -> x31, starting transfers between devices: 45.1 us -> 31.9 us  [swap(): return lax.ppermute(x, axis, [(s, s ^ mask) for s in range(size)])]
    unnamed x104 -> x61, local copies, waits for them, and re-layouts: 13.4 us -> 6.25 us
    dot_general x3 -> x0, matrix products: 6.57 us -> none  [the longest x1 3.28 us: local(): grad_ada = dot('ti,tj->ij', all_act, all_mod)]
  transfers between devices with their start and end apart: 56 -> 51, of which waited for: 20 -> 15; matrix products, arithmetic and copies ran while one was open for 9% -> 9% of each run, Pallas kernels for 40% -> 50%
where the time goes in v2:
time: 280 us; the launch traced here: 275 us
  Pallas kernels  142 us (51%)
  waiting for transfers between devices  50.9 us (18%)
  starting transfers between devices  48.7 us (17%)
  other arithmetic  15.8 us (6%)
  local copies, waits for them, and re-layouts  14.5 us (5%)
    pallas_call x2, Pallas kernels, call_middle(): pl.pallas_call(functools.partial(middle, n, start, not init, last_chunk),...  67.8 us
    ppermute x20, waiting for transfers between devices, swap_by_core(): return lax.ppermute(x, ('frame', 'pack'), perm)  35 us
    ppermute x31, starting transfers between devices, swap(): return lax.ppermute(x, axis, [(s, s ^ mask) for s in range(size)])  31.9 us
    pallas_call x2, Pallas kernels, call_spatial_bwd(): pl.pallas_call(functools.partial(spatial_bwd, n, not init, last_chunk), g...  26.1 us
    pallas_call x2, Pallas kernels, call_spatial_fwd(): pl.pallas_call(functools.partial(spatial_fwd, start), grid_spec=pltpu.Pre...  24.2 us
    ppermute x20, starting transfers between devices, swap_by_core(): return lax.ppermute(x, ('frame', 'pack'), perm)  16.8 us
    ppermute x31, waiting for transfers between devices, swap(): return lax.ppermute(x, axis, [(s, s ^ mask) for s in range(size)])  15.9 us
    pallas_call x2, Pallas kernels, call_last(): pl.pallas_call(functools.partial(last_step, masks), grid_spec=pltpu.Prefe...  13.1 us
  transfers between devices with their start and end apart: 51, of which 15 were waited for; matrix products, arithmetic and copies ran while one was open for 9% of the time, Pallas kernels for 50%

profile of v2, /device:TPU:0, one launch (start us, length us, event | category | flops | bytes accessed | tf_op | source)
XLA Modules:
  0.0 274.8 jit_solution(76078193039701695)
XLA Ops:
  0.7 2.4 constant_dynamic-slice_fusion.8
  3.6 2.5 collective-permute-start
  8.0 12.1 %spatial_fwd.3 = (bf16[2,2,1152,256]{3,2,1,0:T(8,128)(2,1)}, bf16[2,2,384,256]{3,2,1,0:T(8,128)(2,1)}, bf16[2,2,256,384]{3,2,1,0:T(8,128)(2,1)}, f32[2,2,3,512]{...) custom-call(s32[1]{0:T(128)} %bitcast.idx, ...), custom_call_target="tpu_custom_call" | custom-call | flops 12000000000 | bytes 1000 | tf_op jit(solution)/shard_map/spatial_fwd/pallas_call | solution.py:119
  26.6 12.1 %spatial_fwd.2 = (bf16[2,2,1152,256]{3,2,1,0:T(8,128)(2,1)}, bf16[2,2,384,256]{3,2,1,0:T(8,128)(2,1)}, bf16[2,2,256,384]{3,2,1,0:T(8,128)(2,1)}, f32[2,2,3,512]{...) custom-call(s32[1]{0:T(128)} %bitcast.idx, ...), custom_call_target="tpu_custom_call" | custom-call | flops 12000000000 | bytes 1000 | tf_op jit(solution)/shard_map/spatial_fwd/pallas_call | solution.py:119
  40.7 4.4 %collective-permute-done.3.refs_2_ = bf16[2,2,64,384]{3,2,1,0:T(8,128)(2,1)S(1)} collective-permute-done((bf16[2,2,64,384]{3,2,1,0:T(8,128)(2,1)}, bf16[2,2,64,384]{3,2,1,0:T(8,128)(2,1)S(1)}, u32[]{:S(2)}, u32[]{:S(2)}) %collective-permute-start.3) | collective-permute-done | bytes 196640 | tf_op jit(solution)/shard_map/ppermute | solution.py:551
  45.0 2.9 %collective-permute-done.4.refs_3_ = bf16[2,2,64,384]{3,2,1,0:T(8,128)(2,1)S(1)} collective-permute-done((bf16[2,2,64,384]{3,2,1,0:T(8,128)(2,1)}, bf16[2,2,64,384]{3,2,1,0:T(8,128)(2,1)S(1)}, u32[]{:S(2)}, u32[]{:S(2)}) %collective-permute-start.4) | collective-permute-done | bytes 196640 | tf_op jit(solution)/shard_map/ppermute | solution.py:551
  50.0 33.1 %middle.2 = (bf16[2,2,64,384]{3,2,1,0:T(8,128)(2,1)}, bf16[2,2,64,384]{3,2,1,0:T(8,128)(2,1)}, bf16[2,2,64,384]{3,2,1,0:T(8,128)(2,1)}, bf16[2,2,64,384]{3,2,1,0...) custom-call(s32[1]{0:T(128)} %bitcast.idx, ...), custom_call_target="tpu_custom_call" | custom-call | flops 32000000000 | bytes 1000 | tf_op jit(solution)/shard_map/middle/pallas_call | solution.py:329
  86.3 34.8 %middle.3 = (bf16[2,2,64,384]{3,2,1,0:T(8,128)(2,1)}, bf16[2,2,64,384]{3,2,1,0:T(8,128)(2,1)}, bf16[2,2,64,384]{3,2,1,0:T(8,128)(2,1)}, bf16[2,2,64,384]{3,2,1,0...) custom-call(s32[1]{0:T(128)} %bitcast.idx, ...), custom_call_target="tpu_custom_call", output_to_operand_aliasing={{4}: (19, {}), {5}: (20, {})} | custom-call | flops 32000000000 | bytes 1000 | tf_op jit(solution)/shard_map/middle/pallas_call | solution.py:329
  125.8 12.8 %spatial_bwd.2 = (bf16[2,2,1152,256]{3,2,1,0:T(8,128)(2,1)}, f32[2,2,256,384]{3,2,1,0:T(8,128)}, f32[2,2,1,384]{3,2,1,0:T(1,128)}, f32[4,384,384]{2,1,0:T(8,128)}) custom-call(s32[1]{0:T(128)} %bitcast.idx, bf16[4,2,256,384]{3,2,1,0:T(8,128)(2,1)} %tok.10, bf16[4,2,256,384]{3,2,1,0:T(8,128)(2,1)} %cot.3, f32[2,2,3,384]{3,2,1,0:T(4,128)} %get-tuple-element.106.mod, ...), custom_call_target="tpu_custom_call" | custom-call | flops 12000000000 | bytes 1000 | tf_op jit(solution)/shard_map/spatial_bwd/pallas_call | solution.py:429
  143.3 13.3 %spatial_bwd.3 = (bf16[2,2,1152,256]{3,2,1,0:T(8,128)(2,1)}, f32[2,2,256,384]{3,2,1,0:T(8,128)}, f32[2,2,1,384]{3,2,1,0:T(1,128)}, bf16[2,384,384]{2,1,0:T(8,128)(2,1)}, bf16[2,384,384]{2,1,0:T(8,128)(2,1)}) custom-call(s32[1]{0:T(128)} %bitcast.idx, bf16[4,2,256,384]{3,2,1,0:T(8,128)(2,1)} %tok.10, bf16[4,2,256,384]{3,2,1,0:T(8,128)(2,1)} %cot.3, ...), custom_call_target="tpu_custom_call" | custom-call | flops 12000000000 | bytes 1000 | tf_op jit(solution)/shard_map/spatial_bwd/pallas_call | solution.py:429
  166.7 6.4 %last_step.2 = (f32[4,2,256,384]{3,2,1,0:T(8,128)}, bf16[4,2,256,384]{3,2,1,0:T(8,128)(2,1)}, f32[2,2,2,384]{3,2,1,0:T(2,128)}) custom-call(s32[1]{0:T(128)} %bitcast.idx, bf16[4,2,256,384]{3,2,1,0:T(8,128)(2,1)} %tok.10, f32[2,2,3,384]{3,2,1,0:T(4,128)} %get-tuple-element.106.mod, bf16[1152,384]{1,0:T(8,128)(2,1)} %bitcast.39, ...), custom_call_target="tpu_custom_call" | custom-call | flops 6000000000 | bytes 1000 | tf_op jit(solution)/shard_map/last_step/pallas_call | solution.py:475
  178.2 6.7 %last_step.3 = (f32[4,2,256,384]{3,2,1,0:T(8,128)}, bf16[4,2,256,384]{3,2,1,0:T(8,128)(2,1)}, f32[2,2,2,384]{3,2,1,0:T(2,128)}) custom-call(s32[1]{0:T(128)} %bitcast.idx, bf16[4,2,256,384]{3,2,1,0:T(8,128)(2,1)} %tok.10, f32[2,2,3,384]{3,2,1,0:T(4,128)} %get-tuple-element.101.mod, ...), custom_call_target="tpu_custom_call", output_to_operand_aliasing={{0}: (10, {}), {1}: (11, {})} | custom-call | flops 6000000000 | bytes 1000 | tf_op jit(solution)/shard_map/last_step/pallas_call | solution.py:475
  187.4 2.6 collective-permute-start.36
  197.5 5.9 %collective-permute-done.41 = bf16[32,1152]{1,0:T(8,128)(2,1)S(1)} collective-permute-done((bf16[32,1152]{1,0:T(8,128)(2,1)S(1)}, bf16[32,1152]{1,0:T(8,128)(2,1)S(1)}, u32[]{:S(2)}, u32[]{:S(2)}) %collective-permute-start.41) | collective-permute-done | bytes 73760 | tf_op jit(solution)/shard_map/ppermute | solution.py:551
  206.2 3.8 %collective-permute-done.27 = bf16[96,384]{1,0:T(8,128)(2,1)S(1)} collective-permute-done((bf16[96,384]{1,0:T(8,128)(2,1)S(1)}, bf16[96,384]{1,0:T(8,128)(2,1)S(1)}, u32[]{:S(2)}, u32[]{:S(2)}) %collective-permute-start.27) | collective-permute-done | bytes 73760 | tf_op jit(solution)/shard_map/ppermute | solution.py:577
  211.4 2.8 %collective-permute-start.45 = (bf16[144,384]{1,0:T(8,128)(2,1)S(1)}, bf16[144,384]{1,0:T(8,128)(2,1)S(1)}, u32[]{:S(2)}, u32[]{:S(2)}) collective-permute-start(bf16[144,384]{1,0:T(8,128)(2,1)S(1)} %constant_dynamic-slice_fusion), channel_id=1, source_target_pairs={{0,4},{8,24},{16,20},{24,8},{1,5},{9,25},{17,21},{25,9},{2,6},{10,... | collective-permute-start | bytes 331784 | tf_op jit(solution)/shard_map/ppermute | solution.py:577
  215.4 4.4 %collective-permute-start.43 = (bf16[128,1152]{1,0:T(8,128)(2,1)S(1)}, bf16[128,1152]{1,0:T(8,128)(2,1)S(1)}, u32[]{:S(2)}, u32[]{:S(2)}) collective-permute-start(bf16[128,1152]{1,0:T(8,128)(2,1)S(1)} %pad_maximum_fusion.11), channel_id=1, source_target_pairs={{0,8},{8,0},{16,24},{24,16},{1,9},{9,1},{17,25},{25,17},{2,10},{10... | collective-permute-start | bytes 884744 | tf_op jit(solution)/shard_map/ppermute | solution.py:551
  222.4 4.0 %collective-permute-done.46 = bf16[144,384]{1,0:T(8,128)(2,1)S(1)} collective-permute-done((bf16[144,384]{1,0:T(8,128)(2,1)S(1)}, bf16[144,384]{1,0:T(8,128)(2,1)S(1)}, u32[]{:S(2)}, u32[]{:S(2)}) %collective-permute-start.46) | collective-permute-done | bytes 110624 | tf_op jit(solution)/shard_map/ppermute | solution.py:577
  227.7 6.3 %collective-permute-done.47 = bf16[288,384]{1,0:T(8,128)(2,1)S(1)} collective-permute-done((bf16[288,384]{1,0:T(8,128)(2,1)S(1)}, bf16[288,384]{1,0:T(8,128)(2,1)S(1)}, u32[]{:S(2)}, u32[]{:S(2)}) %collective-permute-start.47) | collective-permute-done | bytes 221216 | tf_op jit(solution)/shard_map/ppermute | solution.py:577
  235.6 6.9 %collective-permute-done.48 = bf16[576,384]{1,0:T(8,128)(2,1)S(1)} collective-permute-done((bf16[576,384]{1,0:T(8,128)(2,1)S(1)}, bf16[576,384]{1,0:T(8,128)(2,1)S(1)}, u32[]{:S(2)}, u32[]{:S(2)}) %collective-permute-start.48) | collective-permute-done | bytes 442400 | tf_op jit(solution)/shard_map/ppermute | solution.py:577
  246.0 9.9 %collective-permute-done.49 = bf16[1152,384]{1,0:T(8,128)(2,1)S(1)} collective-permute-done((bf16[1152,384]{1,0:T(8,128)(2,1)S(1)}, bf16[1152,384]{1,0:T(8,128)(2,1)S(1)}, u32[]{:S(2)}, u32[]{:S(2)}) %collective-permute-start.49) | collective-permute-done | bytes 884768 | tf_op jit(solution)/shard_map/ppermute | solution.py:577
  256.5 2.6 collective-permute-done.32
  262.1 5.9 %finish_late.1 = (f32[384,3456]{1,0:T(8,128)}, f32[384,1152]{1,0:T(8,128)}, f32[384,384]{1,0:T(8,128)}) custom-call(s32[1]{0:T(128)} %bitcast.idx, bf16[2,384,384]{2,1,0:T(8,128)(2,1)} %bitcast.43, bf16[2,384,384]{2,1,0:T(8,128)(2,1)} %bitcast.56, bf16[256,2688]{1,0:T(8,128)(2,1)} %pad_maximum_fusion.1.rest, bf16[256,1152]{1,0:T(8,128)(2,1)} %pad_maximum_fusion.6.mod), custom_call_target="tpu_custom_call" | custom-call | flops 4000000000 | bytes 1000 | tf_op jit(solution)/shard_map/finish_late/pallas_call | solution.py:538
  269.3 5.3 %finish_early.1 = (f32[384,1536]{1,0:T(8,128)}, f32[1536,384]{1,0:T(8,128)}, f32[384,1152]{1,0:T(8,128)}, f32[384,384]{1,0:T(8,128)}) custom-call(s32[1]{0:T(128)} %bitcast.idx, bf16[6,384,384]{2,1,0:T(8,128)(2,1)} %bitcast.36, bf16[6,384,384]{2,1,0:T(8,128)(2,1)} %bitcast.54), custom_call_target="tpu_custom_call" | custom-call | flops 3000000000 | bytes 1000 | tf_op jit(solution)/shard_map/finish_early/pallas_call | solution.py:515
  (238 shorter events, 69.4 us)
Async XLA Ops:
  3.1 22.0 %collective-permute-start.1 = (bf16[4,2,64,384]{3,2,1,0:T(8,128)(2,1)S(1)}, bf16[4,2,64,384]{3,2,1,0:T(8,128)(2,1)S(1)}, u32[]{:S(2)}, u32[]{:S(2)}) collective-permute-start(bf16[4,2,64,384]{3,2,1,0:T(8,128)(2,1)S(1)} %get-tuple-element.195), channel_id=1, source_target_pairs={{0,8},{8,0},{16,24},{24,16},{1,9},{9,1},{17,25},{25,17},{2,10},{10... | collective-permute-start | bytes 1179656 | tf_op jit(solution)/shard_map/ppermute | solution.py:551
  3.6 21.1 %collective-permute-start = (bf16[1,4,2,384]{3,2,1,0:T(2,128)(2,1)S(1)}, bf16[1,4,2,384]{3,2,1,0:T(2,128)(2,1)S(1)}, u32[]{:S(2)}, u32[]{:S(2)}) collective-permute-start(bf16[1,4,2,384]{3,2,1,0:T(2,128)(2,1)S(1)} %bitcast.51), channel_id=1, source_target_pairs={{0,16},{8,24},{16,0},{24,8},{1,17},{9,25},{17,1},{25,9},{2,18},{10... | collective-permute-start | bytes 18440 | tf_op jit(solution)/shard_map/ppermute | solution.py:551
  20.2 18.5 %collective-permute-start.2 = (bf16[2,2,64,384]{3,2,1,0:T(8,128)(2,1)}, bf16[2,2,64,384]{3,2,1,0:T(8,128)(2,1)S(1)}, u32[]{:S(2)}, u32[]{:S(2)}) collective-permute-start(bf16[2,2,64,384]{3,2,1,0:T(8,128)(2,1)} %get-tuple-element.112), channel_id=1, source_target_pairs={{0,8},{8,0},{16,24},{24,16},{1,9},{9,1},{17,25},{25,17},{2,10},{10... | collective-permute-start | bytes 589832 | tf_op jit(solution)/shard_map/ppermute | solution.py:551
  20.4 27.5 %collective-permute-start.5 = (bf16[4,2,64,384]{3,2,1,0:T(8,128)(2,1)S(1)}, bf16[4,2,64,384]{3,2,1,0:T(8,128)(2,1)S(1)}, u32[]{:S(2)}, u32[]{:S(2)}) collective-permute-start(bf16[4,2,64,384]{3,2,1,0:T(8,128)(2,1)S(1)} %get-tuple-element.193), channel_id=1, source_target_pairs={{0,16},{8,24},{16,0},{24,8},{1,17},{9,25},{17,1},{25,9},{2,18},{10... | collective-permute-start | bytes 1179656 | tf_op jit(solution)/shard_map/ppermute | solution.py:551
  20.7 27.2 %collective-permute-start.6 = (bf16[4,2,64,384]{3,2,1,0:T(8,128)(2,1)S(1)}, bf16[4,2,64,384]{3,2,1,0:T(8,128)(2,1)S(1)}, u32[]{:S(2)}, u32[]{:S(2)}) collective-permute-start(bf16[4,2,64,384]{3,2,1,0:T(8,128)(2,1)S(1)} %get-tuple-element.192), channel_id=1, source_target_pairs={{0,24},{8,16},{16,8},{24,0},{1,25},{9,17},{17,9},{25,1},{2,26},{10... | collective-permute-start | bytes 1179656 | tf_op jit(solution)/shard_map/ppermute | solution.py:551
  24.6 20.4 %collective-permute-start.3 = (bf16[2,2,64,384]{3,2,1,0:T(8,128)(2,1)}, bf16[2,2,64,384]{3,2,1,0:T(8,128)(2,1)S(1)}, u32[]{:S(2)}, u32[]{:S(2)}) collective-permute-start(bf16[2,2,64,384]{3,2,1,0:T(8,128)(2,1)} %get-tuple-element.113), channel_id=1, source_target_pairs={{0,16},{8,24},{16,0},{24,8},{1,17},{9,25},{17,1},{25,9},{2,18},{10... | collective-permute-start | bytes 589832 | tf_op jit(solution)/shard_map/ppermute | solution.py:551
  25.1 22.9 %collective-permute-start.4 = (bf16[2,2,64,384]{3,2,1,0:T(8,128)(2,1)}, bf16[2,2,64,384]{3,2,1,0:T(8,128)(2,1)S(1)}, u32[]{:S(2)}, u32[]{:S(2)}) collective-permute-start(bf16[2,2,64,384]{3,2,1,0:T(8,128)(2,1)} %get-tuple-element.114), channel_id=1, source_target_pairs={{0,24},{8,16},{16,8},{24,0},{1,25},{9,17},{17,9},{25,1},{2,26},{10... | collective-permute-start | bytes 589832 | tf_op jit(solution)/shard_map/ppermute | solution.py:551
  48.0 35.9 %collective-permute-start.11 = (bf16[2,2,64,384]{3,2,1,0:T(8,128)(2,1)}, bf16[2,2,64,384]{3,2,1,0:T(8,128)(2,1)S(1)}, u32[]{:S(2)}, u32[]{:S(2)}) collective-permute-start(bf16[2,2,64,384]{3,2,1,0:T(8,128)(2,1)} %get-tuple-element.126), channel_id=1, source_target_pairs={{0,8},{8,0},{16,24},{24,16},{1,9},{9,1},{17,25},{25,17},{2,10},{10... | collective-permute-start | bytes 589832 | tf_op jit(solution)/shard_map/ppermute | solution.py:551
  48.5 37.0 %collective-permute-start.12 = (bf16[2,2,64,384]{3,2,1,0:T(8,128)(2,1)}, bf16[2,2,64,384]{3,2,1,0:T(8,128)(2,1)S(1)}, u32[]{:S(2)}, u32[]{:S(2)}) collective-permute-start(bf16[2,2,64,384]{3,2,1,0:T(8,128)(2,1)} %get-tuple-element.127), channel_id=1, source_target_pairs={{0,16},{8,24},{16,0},{24,8},{1,17},{9,25},{17,1},{25,9},{2,18},{10... | collective-permute-start | bytes 589832 | tf_op jit(solution)/shard_map/ppermute | solution.py:551
  48.8 36.7 %collective-permute-start.13 = (bf16[2,2,64,384]{3,2,1,0:T(8,128)(2,1)}, bf16[2,2,64,384]{3,2,1,0:T(8,128)(2,1)S(1)}, u32[]{:S(2)}, u32[]{:S(2)}) collective-permute-start(bf16[2,2,64,384]{3,2,1,0:T(8,128)(2,1)} %get-tuple-element.128), channel_id=1, source_target_pairs={{0,24},{8,16},{16,8},{24,0},{1,25},{9,17},{17,9},{25,1},{2,26},{10... | collective-permute-start | bytes 589832 | tf_op jit(solution)/shard_map/ppermute | solution.py:551
  83.0 38.0 %collective-permute-start.10 = (bf16[2,2,64,384]{3,2,1,0:T(8,128)(2,1)}, bf16[2,2,64,384]{3,2,1,0:T(8,128)(2,1)S(1)}, u32[]{:S(2)}, u32[]{:S(2)}) collective-permute-start(bf16[2,2,64,384]{3,2,1,0:T(8,128)(2,1)} %get-tuple-element.119), channel_id=1, source_target_pairs={{0,24},{8,16},{16,8},{24,0},{1,25},{9,17},{17,9},{25,1},{2,26},{10... | collective-permute-start | bytes 589832 | tf_op jit(solution)/shard_map/ppermute | solution.py:551
  83.7 37.4 %collective-permute-start.8 = (bf16[2,2,64,384]{3,2,1,0:T(8,128)(2,1)}, bf16[2,2,64,384]{3,2,1,0:T(8,128)(2,1)S(1)}, u32[]{:S(2)}, u32[]{:S(2)}) collective-permute-start(bf16[2,2,64,384]{3,2,1,0:T(8,128)(2,1)} %get-tuple-element.117), channel_id=1, source_target_pairs={{0,8},{8,0},{16,24},{24,16},{1,9},{9,1},{17,25},{25,17},{2,10},{10... | collective-permute-start | bytes 589832 | tf_op jit(solution)/shard_map/ppermute | solution.py:551
  83.9 37.2 %collective-permute-start.9 = (bf16[2,2,64,384]{3,2,1,0:T(8,128)(2,1)}, bf16[2,2,64,384]{3,2,1,0:T(8,128)(2,1)S(1)}, u32[]{:S(2)}, u32[]{:S(2)}) collective-permute-start(bf16[2,2,64,384]{3,2,1,0:T(8,128)(2,1)} %get-tuple-element.118), channel_id=1, source_target_pairs={{0,16},{8,24},{16,0},{24,8},{1,17},{9,25},{17,1},{25,9},{2,18},{10... | collective-permute-start | bytes 589832 | tf_op jit(solution)/shard_map/ppermute | solution.py:551
  121.4 20.4 %collective-permute-start.17 = (bf16[2,2,64,384]{3,2,1,0:T(8,128)(2,1)}, bf16[2,2,64,384]{3,2,1,0:T(8,128)(2,1)}, u32[]{:S(2)}, u32[]{:S(2)}) collective-permute-start(bf16[2,2,64,384]{3,2,1,0:T(8,128)(2,1)} %get-tuple-element.151), channel_id=1, source_target_pairs={{0,24},{8,16},{16,8},{24,0},{1,25},{9,17},{17,9},{25,1},{2,26},{10... | collective-permute-start | bytes 589832 | tf_op jit(solution)/shard_map/ppermute | solution.py:551
  121.7 21.6 %collective-permute-start.16 = (bf16[2,2,64,384]{3,2,1,0:T(8,128)(2,1)}, bf16[2,2,64,384]{3,2,1,0:T(8,128)(2,1)}, u32[]{:S(2)}, u32[]{:S(2)}) collective-permute-start(bf16[2,2,64,384]{3,2,1,0:T(8,128)(2,1)} %get-tuple-element.149), channel_id=1, source_target_pairs={{0,16},{8,24},{16,0},{24,8},{1,17},{9,25},{17,1},{25,9},{2,18},{10... | collective-permute-start | bytes 589832 | tf_op jit(solution)/shard_map/ppermute | solution.py:551
  123.3 20.0 %collective-permute-start.15 = (bf16[2,2,64,384]{3,2,1,0:T(8,128)(2,1)}, bf16[2,2,64,384]{3,2,1,0:T(8,128)(2,1)}, u32[]{:S(2)}, u32[]{:S(2)}) collective-permute-start(bf16[2,2,64,384]{3,2,1,0:T(8,128)(2,1)} %get-tuple-element.147), channel_id=1, source_target_pairs={{0,8},{8,0},{16,24},{24,16},{1,9},{9,1},{17,25},{25,17},{2,10},{10... | collective-permute-start | bytes 589832 | tf_op jit(solution)/shard_map/ppermute | solution.py:551
  123.3 33.3 %collective-permute-start.20 = (bf16[2,4,2,64,384]{4,3,2,1,0:T(8,128)(2,1)}, bf16[2,4,2,64,384]{4,3,2,1,0:T(8,128)(2,1)}, u32[]{:S(2)}, u32[]{:S(2)}) collective-permute-start(bf16[2,4,2,64,384]{4,3,2,1,0:T(8,128)(2,1)} %get-tuple-element.161), channel_id=1, source_target_pairs={{0,16},{8,24},{16,0},{24,8},{1,17},{9,25},{17,1},{25,9},{2,18},{10... | collective-permute-start | bytes 2359304 | tf_op jit(solution)/shard_map/ppermute | solution.py:551
  139.3 19.3 %collective-permute-start.23 = (f32[4,2,2,6,384]{4,3,2,0,1:T(8,128)}, f32[4,2,2,6,384]{4,3,2,0,1:T(8,128)}, u32[]{:S(2)}, u32[]{:S(2)}) collective-permute-start(f32[4,2,2,6,384]{4,3,2,0,1:T(8,128)} %slice.55), channel_id=1, source_target_pairs={{0,16},{8,24},{16,0},{24,8},{1,17},{9,25},{17,1},{25,9},{2,18},{10... | collective-permute-start | bytes 442376 | tf_op jit(solution)/shard_map/ppermute | solution.py:551
  141.8 24.0 %collective-permute-start.18 = (bf16[1152,384]{1,0:T(8,128)(2,1)S(1)}, bf16[1152,384]{1,0:T(8,128)(2,1)S(1)}, u32[]{:S(2)}, u32[]{:S(2)}) collective-permute-start(bf16[1152,384]{1,0:T(8,128)(2,1)S(1)} %constant_dynamic-slice_fusion.7), channel_id=1, source_target_pairs={{0,1},{8,10},{16,17},{24,26},{1,0},{9,11},{17,16},{25,27},{2,3},{1... | collective-permute-start | bytes 2654216 | tf_op jit(solution)/shard_map/ppermute | solution.py:577
  177.8 32.6 %collective-permute-start.44 = (bf16[288,384]{1,0:T(8,128)(2,1)}, bf16[288,384]{1,0:T(8,128)(2,1)}, u32[]{:S(2)}, u32[]{:S(2)}) collective-permute-start(bf16[288,384]{1,0:T(8,128)(2,1)} %constant_dynamic-slice_fusion.5), channel_id=1, source_target_pairs={{0,2},{8,9},{16,18},{24,25},{1,3},{9,8},{17,19},{25,24},{2,0},{10,... | collective-permute-start | bytes 663560 | tf_op jit(solution)/shard_map/ppermute | solution.py:577
  187.4 18.3 %collective-permute-start.36 = (bf16[32,2688]{1,0:T(8,128)(2,1)}, bf16[32,2688]{1,0:T(8,128)(2,1)S(1)}, u32[]{:S(2)}, u32[]{:S(2)}) collective-permute-start(bf16[32,2688]{1,0:T(8,128)(2,1)} %pad_maximum_fusion.13), channel_id=1, source_target_pairs={{0,4},{1,5},{2,6},{3,7},{4,0},{5,1},{6,2},{7,3},{8,12},{9,13},{10,... | collective-permute-start | bytes 516104 | tf_op jit(solution)/shard_map/ppermute | solution.py:551
  205.8 29.5 %collective-permute-start.37 = (bf16[64,2688]{1,0:T(8,128)(2,1)S(1)}, bf16[64,2688]{1,0:T(8,128)(2,1)S(1)}, u32[]{:S(2)}, u32[]{:S(2)}) collective-permute-start(bf16[64,2688]{1,0:T(8,128)(2,1)S(1)} %pad_maximum_fusion.9), channel_id=1, source_target_pairs={{0,16},{8,24},{16,0},{24,8},{1,17},{9,25},{17,1},{25,9},{2,18},{10... | collective-permute-start | bytes 1032200 | tf_op jit(solution)/shard_map/ppermute | solution.py:551
  215.4 29.6 %collective-permute-start.43 = (bf16[128,1152]{1,0:T(8,128)(2,1)S(1)}, bf16[128,1152]{1,0:T(8,128)(2,1)S(1)}, u32[]{:S(2)}, u32[]{:S(2)}) collective-permute-start(bf16[128,1152]{1,0:T(8,128)(2,1)S(1)} %pad_maximum_fusion.11), channel_id=1, source_target_pairs={{0,8},{8,0},{16,24},{24,16},{1,9},{9,1},{17,25},{25,17},{2,10},{10... | collective-permute-start | bytes 884744 | tf_op jit(solution)/shard_map/ppermute | solution.py:551
  235.5 23.8 %collective-permute-start.38 = (bf16[128,2688]{1,0:T(8,128)(2,1)S(1)}, bf16[128,2688]{1,0:T(8,128)(2,1)S(1)}, u32[]{:S(2)}, u32[]{:S(2)}) collective-permute-start(bf16[128,2688]{1,0:T(8,128)(2,1)S(1)} %pad_maximum_fusion.4), channel_id=1, source_target_pairs={{0,8},{8,0},{16,24},{24,16},{1,9},{9,1},{17,25},{25,17},{2,10},{10... | collective-permute-start | bytes 2064392 | tf_op jit(solution)/shard_map/ppermute | solution.py:551
  (55 other events, 432.1 us)
